TPU v7x, 128 devices: a whole 4x4x4 slice. The times are simulated.
128 devices in a mesh: lon: 8 (over z, x_hi), lat: 16 (over y, x_lo, core).
Axes of the slice: x: 4 (x_hi: 2, x_lo: 2; x = x_hi * 2 + x_lo), y: 4, z: 4, core: 2. Of those that a mesh axis runs over, the one named last changes fastest.
Arguments:
- state_field: bfloat16 [192, 128, 1024], P(None, 'lat', 'lon'), may hold values from -6 to 6
- depth_kernel: float32 [192, 49], replicated, may hold values from -0.875 to 0.875
- norm_gain: float32 [192], replicated, may hold values from 0.25 to 1.75
- w_expand: bfloat16 [192, 768], replicated, may hold values from -0.4375 to 0.4375
- w_project: bfloat16 [768, 192], replicated, may hold values from -0.21875 to 0.21875
- layer_scale: float32 [192], replicated, may hold values from 0.5 to 1.5
- cotangent: bfloat16 [192, 128, 1024], P(None, 'lat', 'lon'), may hold values from -6 to 6
- send_cells: int32 [16, 8192], P('lat', 'lon'), may hold values from 0 to 1023, as said below
- send_count: int32 [16, 128], P('lat', 'lon'), may hold values from 4 to 64, as said below
- fold_partner: int32 [1024], replicated, may hold values from 0 to 1023, each once
Outputs:
- out_field: bfloat16 [192, 128, 1024], P(None, 'lat', 'lon')
- grad_field: bfloat16 [192, 128, 1024], P(None, 'lat', 'lon')
- grad_kernel: float32 [192, 49], replicated
- grad_expand: float32 [192, 768], replicated
- grad_project: float32 [768, 192], replicated
Inputs may be any that keep to these rules, and one draw needn't show every extreme that they name: `send_cells`: the entries of one device's row are distinct. `send_count`: A device has equally many live slots in every slot block. In every sector the devices of the 16 bands, in a drawn order, have 64 // 16 times 1, 2, ..., 16 live slots in each block.
All inputs are finite; a program needn't handle non-finite values.
Results may differ from a plain program's by a relative error of at most 0.0075.
Values may be sent and summed in bfloat16 or wider, within the bound.
A program may use at most 64 MiB of HBM per device.

v0:
```python
import jax
import jax.numpy as jnp
from jax import lax
from jax.sharding import PartitionSpec as P

root_half = 0.7071067811865476
root_twopi_inv = 0.3989422804014327


def padded_2(x, sides, width):
    for axis, dim in sides:
        peers, length = (lax.axis_size(axis), x.shape[dim])
        up = [(i, (i + 1) % peers) for i in range(peers)]
        down = [(j, i) for i, j in up]
        last = lax.slice_in_dim(x, length - width, length, axis=dim)
        leading = lax.slice_in_dim(x, 0, width, axis=dim)
        before = lax.ppermute(last, axis, up)
        after = lax.ppermute(leading, axis, down)
        x = jnp.concatenate([before, x, after], axis=dim)
    return x


def gelu_value(pre_act):
    return 0.5 * pre_act * (1.0 + jax.scipy.special.erf(pre_act * root_half))


def gelu_slope(pre_act):
    return (
        0.5 * (1.0 + jax.scipy.special.erf(pre_act * root_half))
        + pre_act * jnp.exp(-0.5 * pre_act * pre_act) * root_twopi_inv
    )


def forward_rows(row_block, norm_gain, w_expand, w_project):
    values = row_block.astype(jnp.float32)
    center = values - jnp.mean(values, axis=0, keepdims=True)
    variance = jnp.mean(center * center, axis=0, keepdims=True)
    inv_std = lax.rsqrt(variance + 1e-06)
    normed = center * inv_std
    scaled = (normed * norm_gain[:, None]).astype(jnp.bfloat16)
    pre_act = lax.dot_general(
        w_expand, scaled, (((0,), (0,)), ((), ())), preferred_element_type=jnp.float32
    )
    hidden = gelu_value(pre_act).astype(jnp.bfloat16)
    output = lax.dot_general(
        w_project, hidden, (((0,), (0,)), ((), ())), preferred_element_type=jnp.float32
    )
    return (output.astype(jnp.bfloat16), (normed, inv_std, scaled, pre_act, hidden))


def backward_rows(stored, upstream, norm_gain, w_expand, w_project):
    normed, inv_std, scaled, pre_act, hidden = stored
    grad_hidden = jnp.dot(w_project, upstream, preferred_element_type=jnp.float32)
    grad_pre = (grad_hidden * gelu_slope(pre_act)).astype(jnp.bfloat16)
    grad_project = lax.dot_general(
        hidden, upstream, (((1,), (1,)), ((), ())), preferred_element_type=jnp.float32
    )
    grad_expand = lax.dot_general(
        scaled, grad_pre, (((1,), (1,)), ((), ())), preferred_element_type=jnp.float32
    )
    grad_scaled = jnp.dot(w_expand, grad_pre, preferred_element_type=jnp.float32)
    grad_normed = grad_scaled * norm_gain[:, None]
    grad_rows = inv_std * (
        grad_normed
        - jnp.mean(grad_normed, axis=0, keepdims=True)
        - normed * jnp.mean(grad_normed * normed, axis=0, keepdims=True)
    )
    return (grad_rows.astype(jnp.bfloat16), grad_expand, grad_project)


def extend(tile, north_fill, is_south, is_north):
    widened = padded_2(tile, (("lon", 2), ("lat", 1)), 3)
    lat_cells = tile.shape[1]
    south_rows = jnp.where(is_south, jnp.zeros_like(widened[:, :3]), widened[:, :3])
    north_rows = jnp.where(is_north, north_fill, widened[:, lat_cells + 3 :])
    return jnp.concatenate([south_rows, widened[:, 3 : lat_cells + 3], north_rows], axis=1)


def on_device(
    state_field,
    depth_kernel,
    norm_gain,
    w_expand,
    w_project,
    layer_scale,
    cotangent,
    send_cells,
    send_count,
    fold_partner,
):
    channels, lat_cells, lon_cells = state_field.shape
    band_count = lax.axis_size("lat")
    sector_count = lax.axis_size("lon")
    band_index = lax.axis_index("lat")
    sector_index = lax.axis_index("lon")
    is_south = band_index == 0
    is_north = band_index == band_count - 1
    total_lon = lon_cells * sector_count
    cell_list = send_cells[0]
    slot_total = cell_list.shape[0]
    capacity = slot_total // band_count
    live_mask = (
        jnp.arange(slot_total, dtype=jnp.int32) % capacity
        < jnp.repeat(send_count[0], capacity, total_repeat_length=slot_total)
    ).astype(jnp.float32)
    top_rows = state_field[:, lat_cells - 3 :, :]
    gathered = lax.all_gather(top_rows, "lon", axis=2, tiled=True)
    ext_cols = (
        sector_index * lon_cells + jnp.arange(lon_cells + 6, dtype=jnp.int32) - 3
    ) % total_lon
    fold_rows = gathered[:, ::-1, :][:, :, fold_partner[ext_cols]]
    extended = extend(state_field, fold_rows, is_south, is_north)
    ext_f32 = extended.astype(jnp.float32)
    convolved = jnp.zeros((channels, lat_cells, lon_cells), jnp.float32)
    for row_off in range(7):
        for col_off in range(7):
            convolved = (
                convolved
                + depth_kernel[:, 7 * row_off + col_off][:, None, None]
                * ext_f32[:, row_off : row_off + lat_cells, col_off : col_off + lon_cells]
            )
    rounded = convolved.astype(jnp.bfloat16).reshape(channels, lat_cells * lon_cells)
    packed = jnp.take(rounded, cell_list, axis=1)
    cot_rows = jnp.take(cotangent.reshape(channels, lat_cells * lon_cells), cell_list, axis=1)
    upstream_home = (
        live_mask[None, :] * layer_scale[:, None] * cot_rows.astype(jnp.float32)
    ).astype(jnp.bfloat16)
    returned, stored = forward_rows(packed, norm_gain, w_expand, w_project)
    grad_home, grad_expand, grad_project = backward_rows(
        stored, upstream_home, norm_gain, w_expand, w_project
    )
    branch = live_mask[None, :] * layer_scale[:, None] * returned.astype(jnp.float32)
    out_flat = state_field.reshape(channels, -1).astype(jnp.float32).at[:, cell_list].add(branch)
    out_field = out_flat.astype(jnp.bfloat16).reshape(channels, lat_cells, lon_cells)
    grad_conv = (
        jnp.zeros((channels, lat_cells * lon_cells), jnp.bfloat16).at[:, cell_list].set(grad_home)
    )
    grad_conv = grad_conv.reshape(channels, lat_cells, lon_cells)
    grad_ext = extend(
        grad_conv, jnp.zeros((channels, 3, lon_cells + 6), jnp.bfloat16), is_south, is_north
    )
    padded = jnp.concatenate(
        [grad_ext, jnp.zeros((channels, 3, lon_cells + 6), jnp.bfloat16)], axis=1
    ).astype(jnp.float32)
    adjoint = jnp.zeros((channels, lat_cells + 3, lon_cells), jnp.float32)
    for row_off in range(7):
        for col_off in range(7):
            adjoint = (
                adjoint
                + depth_kernel[:, 7 * row_off + col_off][:, None, None]
                * padded[
                    :,
                    6 - row_off : 6 - row_off + lat_cells + 3,
                    6 - col_off : 6 - col_off + lon_cells,
                ]
            )
    fold_term = adjoint[:, lat_cells : lat_cells + 3, :]
    fold_all = lax.all_gather(fold_term.astype(jnp.bfloat16), "lon", axis=2, tiled=True).astype(
        fold_term.dtype
    )
    inverse = (
        jnp.zeros((total_lon,), jnp.int32)
        .at[fold_partner]
        .set(jnp.arange(total_lon, dtype=jnp.int32))
    )
    own_cols = sector_index * lon_cells + jnp.arange(lon_cells, dtype=jnp.int32)
    fold_share = fold_all[:, :, inverse[own_cols]][:, ::-1, :]
    grad_f32 = cotangent.astype(jnp.float32) + adjoint[:, :lat_cells, :]
    grad_f32 = grad_f32.at[:, lat_cells - 3 :, :].add(jnp.where(is_north, fold_share, 0.0))
    grad_field = grad_f32.astype(jnp.bfloat16)
    grad_conv_f32 = grad_conv.astype(jnp.float32)
    kernel_terms = []
    for row_off in range(7):
        for col_off in range(7):
            kernel_terms.append(
                jnp.sum(
                    ext_f32[:, row_off : row_off + lat_cells, col_off : col_off + lon_cells]
                    * grad_conv_f32,
                    axis=(1, 2),
                )
            )
    kernel_local = jnp.stack(kernel_terms, axis=1)
    grad_kernel, grad_expand, grad_project = lax.psum(
        (kernel_local, grad_expand, grad_project), ("lon", "lat")
    )
    return (out_field, grad_field, grad_kernel, grad_expand, grad_project)


def solution(mesh):
    return jax.shard_map(
        on_device,
        mesh=mesh,
        in_specs=(
            P(None, "lat", "lon"),
            P(),
            P(),
            P(),
            P(),
            P(),
            P(None, "lat", "lon"),
            P("lat", "lon"),
            P("lat", "lon"),
            P(),
        ),
        out_specs=(P(None, "lat", "lon"), P(None, "lat", "lon"), P(), P(), P()),
        check_vma=False,
    )
```

profile of v0, /device:TPU:1, one launch (start us, length us, event | category | flops | bytes accessed | tf_op | source)
XLA Modules:
  0.0 434.6 jit_solution(16798975321386561693)
XLA Ops:
  8.8 3.6 collective-permute-start
  12.5 3.6 collective-permute-start.1
  23.9 4.3 scatter_custom_fusion.2
  29.2 4.5 %compare_select_fusion.2 = (s32[1024,1]{0,1:T(1,128)S(1)}, s32[1024,1]{0,1:T(1,128)S(1)}) fusion(s32[]{:T(128)} %bitcast.16, s32[]{:T(128)} %bitcast.17, s32[]{:T(128)} %bitcast.18, s32[]{:T(128)} %bitcast.19, s32[]{:T(128)} %bitcast.20, s32[]{:T(128)} %bitcast.22, s32[]{:T(128)} %bitcast.21, s32[1024,1]{0,1:T(1,128)S(1)} %bitcast.222, ...), kind=kLoop, calls=%fused_computation.266 | loop fusion | flops 14336 | bytes 16412 | tf_op jit(solution)/shard_map/jit(_take)/gather | solution.py:104
  34.5 6.2 %fusion.137 = f32[1024]{0:T(1024)} fusion(pred[1024]{0:T(1024)(128)(4,1)S(1)} %get-tuple-element.112, pred[1024]{0:T(1024)(128)(4,1)S(1)} %get-tuple-element.111, pred[1024]{0:T(1024)(128)(4,1)S(1)} %get-tuple-element.110, pred[1024]{0:T(1024)(128)(4,1)S(1)} %get-tuple-element.109, pred[1024]{0:T(1024)(128)(4,1)S(1)} %get-tuple-element.108, ...), kind=kLoop, calls=%fused_computation.300 | loop fusion | flops 26624 | bytes 21572 | tf_op jit(solution)/shard_map/convert_element_type | solution.py:105
  46.1 3.9 gather_fusion.5
  52.9 10.5 %all-gather.3.cloned.1.call-done = bf16[192,3,1024]{2,0,1:T(8,128)(2,1)} async-done(((bf16[192,3,128]{2,0,1:T(8,128)(2,1)}), bf16[192,3,1024]{2,0,1:T(8,128)(2,1)}) %all-gather.3.cloned.1.call-update) | async-done | bytes 1179664 | tf_op jit(solution)/shard_map/all_gather | solution.py:107
  63.4 2.9 copy.88
  66.2 7.4 %rev.6 = bf16[192,3,1024]{0,1,2:T(4,128)(2,1)} reverse(bf16[192,3,1024]{0,1,2:T(4,128)(2,1)S(1)} %copy.88), dimensions={1} | reverse | bytes 2359296 | tf_op jit(solution)/shard_map/rev | solution.py:111
  73.6 2.5 gather_fusion.1
  79.7 8.7 %add_convert_fusion = bf16[192,8,128]{0,1,2:T(8,128)(2,1)S(1)} fusion(f32[192,14,134]{0,1,2:T(8,128)S(1)} %maximum_convert_fusion.1, f32[192]{0:T(256)S(1)} %bitcast.243, f32[192]{0:T(256)S(1)} %bitcast.245, f32[192]{0:T(256)S(1)} %bitcast.249, f32[192]{0:T(256)S(1)} %bitcast.251, f32[192]{0:T(256)S(1)} %bitcast.253, f32[192]{0:T(256)S(1)} %bitcast.255, ...), kind=kLoop, calls=%fused_computation.227 | loop fusion | flops 19267584 | bytes 38966016 | tf_op jit(solution)/shard_map/convert_element_type | solution.py:122
  89.3 5.7 %gather_fusion.4 = bf16[1024,192]{1,0:T(8,128)(2,1)} fusion(bf16[192,1024]{0,1:T(8,128)(2,1)} %bitcast.209, s32[1024]{0:T(1024)S(1)} %fusion.138), kind=kCustom, calls=%fused_computation.clone | custom fusion | bytes 790528 | tf_op jit(solution)/shard_map/jit(_take)/gather | solution.py:123
  99.3 3.1 fusion.7
  104.3 2.2 fusion.117
  108.4 2.2 fusion.123
  112.6 6.1 %scatter_custom_fusion.1 = bf16[192,1024]{0,1:T(8,128)(2,1)} fusion(s32[1024]{0:T(1024)S(1)} %bitcast.219, bf16[1024,192]{1,0:T(8,128)(2,1)} %copy.96, bf16[]{:T(256)} %constant.185.clone.1), kind=kCustom, calls=%fused_computation.252 | custom fusion | bytes 393728 | tf_op jit(solution)/shard_map/scatter | solution.py:136
  120.3 3.6 fusion.74
  123.9 4.7 %collective-permute-start.5 = (bf16[192,8,3]{0,1,2:T(8,128)(2,1)S(1)}, bf16[192,8,3]{0,1,2:T(8,128)(2,1)S(1)}, u32[]{:S(2)}, u32[]{:S(2)}) collective-permute-start(bf16[192,8,3]{0,1,2:T(8,128)(2,1)S(1)} %copy.165), channel_id=1, source_target_pairs={{16,0},{32,16},{48,32},{64,48},{80,64},{96,80},{112,96},{0,112},{1... | collective-permute-start | bytes 27656 | tf_op jit(solution)/shard_map/ppermute | solution.py:18
  129.6 4.2 collective-permute-start.6
  137.3 4.9 %collective-permute-done.7 = bf16[192,3,134]{0,1,2:T(4,128)(2,1)S(1)} collective-permute-done((bf16[192,3,134]{0,1,2:T(4,128)(2,1)S(1)}, bf16[192,3,134]{0,1,2:T(4,128)(2,1)S(1)}, u32[]{:S(2)}, u32[]{:S(2)}) %collective-permute-start.7) | collective-permute-done | bytes 154400 | tf_op jit(solution)/shard_map/ppermute | solution.py:18
  142.4 3.1 maximum_convert_fusion
  145.5 75.6 %fusion.10 = f32[192,11,128]{0,1,2:T(8,128)} fusion(f32[192,17,134]{0,1,2:T(8,128)} %maximum_convert_fusion, f32[192]{0:T(256)} %bitcast.242, f32[192]{0:T(256)} %bitcast.244, f32[192]{0:T(256)} %bitcast.248, f32[192]{0:T(256)} %bitcast.250, f32[192]{0:T(256)} %bitcast.252, f32[192]{0:T(256)} %bitcast.254, f32[192]{0:T(256)} %bitcast.256, f32[192]{0:T(256)} %bitcast.258, ...), kind=kLoop, calls=%fused_computation.72 | loop fusion | flops 26222592 | bytes 54104832 | tf_op jit(solution)/shard_map/add | solution.py:149
  225.2 2.9 fusion.126
  228.1 5.0 %fusion.92 = (f32[192]{0:T(256)S(1)}, f32[192]{0:T(256)S(1)}, f32[192]{0:T(256)}, f32[192]{0:T(256)}, f32[192]{0:T(256)}, /*index=5*/f32[192]{0:T(256)}, f32[192...) fusion(f32[192,14,134]{0,1,2:T(8,128)S(1)} %maximum_convert_fus, ...), kind=kLoop, calls=%fused_computation.207 | loop fusion | flops 7271040 | bytes 14562816 | tf_op jit(solution)/shard_map/reduce_sum | solution.py:176
  233.0 3.9 fusion.110
  239.5 6.5 %scatter_fusion = f32[192,1024]{0,1:T(8,128)S(1)} fusion(f32[192,1024]{0,1:T(8,128)S(1)} %bitcast.207, s32[1024]{0:T(1024)S(1)} %bitcast.220, f32[1024,192]{1,0:T(8,128)S(1)} %copy.92), kind=kCustom, calls=%fused_computation.6 | custom fusion | flops 196608 | bytes 2363392 | tf_op jit(solution)/shard_map/scatter-add | solution.py:133
  249.4 2.9 stack.199
  252.2 69.4 %psum.21 = f32[192,49]{0,1:T(8,128)} all-reduce(f32[192,49]{0,1:T(8,128)S(1)} %stack.199), channel_id=1, replica_groups=mesh['lon'=8,'lat'=16] {'lon','lat'}, use_global_device_ids=true, to_apply=%region_56.58 | all-reduce | flops 9408 | bytes 75264 | tf_op jit(solution)/shard_map/psum | solution.py:183
  322.9 4.3 copy.102
  327.2 3.2 gather_fusion.3
  331.4 3.4 scatter-add.11
  336.1 87.9 %all-reduce.3.cloned.1.call-done = (f32[192,768]{1,0:T(8,128)}, f32[768,192]{0,1:T(8,128)}) async-done(((f32[192,768]{1,0:T(8,128)}, f32[768,192]{0,1:T(8,128)}), (f32[192,768]{1,0:T(8,128)}, f32[768,192]{0,1:T(8,128)})) %all-reduce.3.cloned.1.call-update) | async-done | bytes 1179664 | tf_op jit(solution)/shard_map/psum | solution.py:183
  (273 shorter events, 56.3 us)
Async XLA Ops:
  7.2 92.1 %copy-start = (bf16[192,768]{1,0:T(8,128)(2,1)S(1)}, bf16[192,768]{1,0:T(8,128)(2,1)}, u32[]{:S(2)}) copy-start(bf16[192,768]{1,0:T(8,128)(2,1)} %param.19) | copy-start | bytes 884740
  7.2 16.7 %copy-start.18 = (s32[8,128]{1,0:T(8,128)S(1)}, s32[8,128]{1,0:T(8,128)}, u32[]{:S(2)}) copy-start(s32[8,128]{1,0:T(8,128)} %constant.180.clone.1) | copy-start | bytes 12292
  7.2 14.7 %copy-start.1 = (s32[1024]{0:T(1024)S(1)}, s32[1024]{0:T(1024)}, u32[]{:S(2)}) copy-start(s32[1024]{0:T(1024)} %param.25) | copy-start | bytes 12292
  7.2 15.9 %copy-start.12 = (s32[1,16]{1,0:T(1,128)S(1)}, s32[1,16]{1,0:T(1,128)}, u32[]{:S(2)}) copy-start(s32[1,16]{1,0:T(1,128)} %param.24) | copy-start | bytes 196
  7.2 26.6 %copy-start.14 = (f32[192,49]{0,1:T(8,128)S(1)}, f32[192,49]{0,1:T(8,128)}, u32[]{:S(2)}) copy-start(f32[192,49]{0,1:T(8,128)} %param.17) | copy-start | bytes 112900
  7.2 56.1 %all-gather.3.cloned.1.call-start = ((), (), s32[]{:S(2)}) async-start(), calls=%async_computation | async-start | bytes 1327104 | tf_op jit(solution)/shard_map/all_gather | solution.py:107
  8.8 34.2 %copy-start.7 = (bf16[192,8,128]{0,1,2:T(8,128)(2,1)}, bf16[192,8,128]{0,1,2:T(8,128)(2,1)S(1)}, u32[]{:S(2)}) copy-start(bf16[192,8,128]{0,1,2:T(8,128)(2,1)S(1)} %copy.84) | copy-start | bytes 1179652
  8.8 33.2 %collective-permute-start = (bf16[192,8,3]{0,1,2:T(8,128)(2,1)S(1)}, bf16[192,8,3]{0,1,2:T(8,128)(2,1)S(1)}, u32[]{:S(2)}, u32[]{:S(2)}) collective-permute-start(bf16[192,8,3]{0,1,2:T(8,128)(2,1)S(1)} %get-tuple-element.123), channel_id=1, source_target_pairs={{0,16},{16,32},{32,48},{48,64},{64,80},{80,96},{96,112},{112,0},{1... | collective-permute-start | bytes 27656 | tf_op jit(solution)/shard_map/ppermute | solution.py:17
  12.5 29.5 %collective-permute-start.1 = (bf16[192,8,3]{0,1,2:T(8,128)(2,1)S(1)}, bf16[192,8,3]{0,1,2:T(8,128)(2,1)S(1)}, u32[]{:S(2)}, u32[]{:S(2)}) collective-permute-start(bf16[192,8,3]{0,1,2:T(8,128)(2,1)S(1)} %get-tuple-element.124), channel_id=1, source_target_pairs={{16,0},{32,16},{48,32},{64,48},{80,64},{96,80},{112,96},{0,112},{1... | collective-permute-start | bytes 27656 | tf_op jit(solution)/shard_map/ppermute | solution.py:18
  17.9 26.4 %copy-start.9 = (bf16[192,8,128]{2,1,0:T(8,128)(2,1)S(1)}, bf16[192,8,128]{2,1,0:T(8,128)(2,1)}, u32[]{:S(2)}) copy-start(bf16[192,8,128]{2,1,0:T(8,128)(2,1)} %param.22) | copy-start | bytes 1179652
  17.9 305.0 %all-gather.5.cloned.1.call-start = ((), (), s32[]{:S(2)}) async-start(), calls=%async_computation.1 | async-start | bytes 1327104 | tf_op jit(solution)/shard_map/all_gather | solution.py:158
  34.5 11.4 %copy-start.8 = (bf16[192,8,128]{2,1,0:T(8,128)(2,1)S(1)}, bf16[192,8,128]{2,1,0:T(8,128)(2,1)}, u32[]{:S(2)}) copy-start(bf16[192,8,128]{2,1,0:T(8,128)(2,1)} %param.16) | copy-start | bytes 1179652
  43.1 9.0 %collective-permute-start.2 = (bf16[192,3,134]{0,1,2:T(4,128)(2,1)S(1)}, bf16[192,3,134]{0,1,2:T(4,128)(2,1)S(1)}, u32[]{:S(2)}, u32[]{:S(2)}) collective-permute-start(bf16[192,3,134]{0,1,2:T(4,128)(2,1)S(1)} %get-tuple-element.119), channel_id=1, source_target_pairs={{0,1},{1,2},{2,3},{3,4},{4,5},{5,6},{6,7},{7,8},{8,9},{9,10},{10,1... | collective-permute-start | bytes 463112 | tf_op jit(solution)/shard_map/ppermute | solution.py:17
  51.6 24.9 %collective-permute-start.3 = (bf16[192,3,134]{0,1,2:T(4,128)(2,1)}, bf16[192,3,134]{0,1,2:T(4,128)(2,1)}, u32[]{:S(2)}, u32[]{:S(2)}) collective-permute-start(bf16[192,3,134]{0,1,2:T(4,128)(2,1)} %get-tuple-element.120), channel_id=1, source_target_pairs={{1,0},{2,1},{3,2},{4,3},{5,4},{6,5},{7,6},{8,7},{9,8},{10,9},{11,1... | collective-permute-start | bytes 463112 | tf_op jit(solution)/shard_map/ppermute | solution.py:18
  76.1 3.2 copy-start.22
  76.1 3.2 copy-start.24
  76.1 3.2 copy-start.25
  89.3 7.7 %copy-start.19 = (pred[1024]{0:T(1024)(128)(4,1)S(1)}, pred[1024]{0:T(1024)(128)(4,1)}, u32[]{:S(2)}) copy-start(pred[1024]{0:T(1024)(128)(4,1)} %compare_and_fusion) | copy-start | bytes 3076
  106.5 6.1 %copy-start.15 = (s32[1024,1]{0,1:T(1,128)S(1)}, s32[1024,1]{0,1:T(1,128)}, u32[]{:S(2)}) copy-start(s32[1024,1]{0,1:T(1,128)} %compare_select_fusion.1) | copy-start | bytes 12292
  119.6 9.0 %copy-start.2 = (bf16[192,1024]{0,1:T(8,128)(2,1)S(1)}, bf16[192,1024]{0,1:T(8,128)(2,1)}, u32[]{:S(2)}) copy-start(bf16[192,1024]{0,1:T(8,128)(2,1)} %scatter_custom_fusion.1) | copy-start | bytes 1179652
  119.6 9.0 %collective-permute-start.4 = (bf16[192,8,3]{0,1,2:T(8,128)(2,1)S(1)}, bf16[192,8,3]{0,1,2:T(8,128)(2,1)S(1)}, u32[]{:S(2)}, u32[]{:S(2)}) collective-permute-start(bf16[192,8,3]{0,1,2:T(8,128)(2,1)S(1)} %copy.164), channel_id=1, source_target_pairs={{0,16},{16,32},{32,48},{48,64},{64,80},{80,96},{96,112},{112,0},{1... | collective-permute-start | bytes 27656 | tf_op jit(solution)/shard_map/ppermute | solution.py:17
  123.9 9.9 %copy-start.5 = (bf16[1024,192]{0,1:T(8,128)(2,1)S(1)}, bf16[1024,192]{0,1:T(8,128)(2,1)}, u32[]{:S(2)}) copy-start(bf16[1024,192]{0,1:T(8,128)(2,1)} %copy.91) | copy-start | bytes 1179652
  123.9 9.9 %copy-start.21 = (pred[1024]{0:T(1024)(128)(4,1)S(1)}, pred[1024]{0:T(1024)(128)(4,1)}, u32[]{:S(2)}) copy-start(pred[1024]{0:T(1024)(128)(4,1)} %compare_and_fusion) | copy-start | bytes 3076
  123.9 9.9 %copy-start.90 = (f32[192]{0:T(256)S(1)}, f32[192]{0:T(256)}, u32[]{:S(2)}) copy-start(f32[192]{0:T(256)} %param.18) | copy-start | bytes 2308
  123.9 9.9 %copy-start.92 = (bf16[768,1024]{0,1:T(8,128)(2,1)S(1)}, bf16[768,1024]{0,1:T(8,128)(2,1)}, u32[]{:S(2)}) copy-start(bf16[768,1024]{0,1:T(8,128)(2,1)} %copy-done.91) | copy-start | bytes 4718596
  123.9 5.5 %collective-permute-start.5 = (bf16[192,8,3]{0,1,2:T(8,128)(2,1)S(1)}, bf16[192,8,3]{0,1,2:T(8,128)(2,1)S(1)}, u32[]{:S(2)}, u32[]{:S(2)}) collective-permute-start(bf16[192,8,3]{0,1,2:T(8,128)(2,1)S(1)} %copy.165), channel_id=1, source_target_pairs={{16,0},{32,16},{48,32},{64,48},{80,64},{96,80},{112,96},{0,112},{1... | collective-permute-start | bytes 27656 | tf_op jit(solution)/shard_map/ppermute | solution.py:18
  129.6 7.6 %collective-permute-start.6 = (bf16[192,3,134]{0,1,2:T(4,128)(2,1)S(1)}, bf16[192,3,134]{0,1,2:T(4,128)(2,1)S(1)}, u32[]{:S(2)}, u32[]{:S(2)}) collective-permute-start(bf16[192,3,134]{0,1,2:T(4,128)(2,1)S(1)} %get-tuple-element.117), channel_id=1, source_target_pairs={{0,1},{1,2},{2,3},{3,4},{4,5},{5,6},{6,7},{7,8},{8,9},{9,10},{10,1... | collective-permute-start | bytes 463112 | tf_op jit(solution)/shard_map/ppermute | solution.py:17
  135.1 7.1 %collective-permute-start.7 = (bf16[192,3,134]{0,1,2:T(4,128)(2,1)S(1)}, bf16[192,3,134]{0,1,2:T(4,128)(2,1)S(1)}, u32[]{:S(2)}, u32[]{:S(2)}) collective-permute-start(bf16[192,3,134]{0,1,2:T(4,128)(2,1)S(1)} %get-tuple-element.118), channel_id=1, source_target_pairs={{1,0},{2,1},{3,2},{4,3},{5,4},{6,5},{7,6},{8,7},{9,8},{10,9},{11,1... | collective-permute-start | bytes 463112 | tf_op jit(solution)/shard_map/ppermute | solution.py:18
  145.5 79.7 %copy-start.17 = (f32[1024]{0:T(1024)S(1)}, f32[1024]{0:T(1024)}, u32[]{:S(2)}) copy-start(f32[1024]{0:T(1024)} %fusion.137) | copy-start | bytes 12292
  224.9 199.1 %all-reduce.3.cloned.1.call-start = ((), (), s32[]{:S(2)}) async-start(), calls=%async_computation.2 | async-start | bytes 2359296 | tf_op jit(solution)/shard_map/psum | solution.py:183
  228.1 5.0 %copy-start.3 = (bf16[192,1024]{0,1:T(8,128)(2,1)S(1)}, bf16[192,1024]{0,1:T(8,128)(2,1)}, u32[]{:S(2)}) copy-start(bf16[192,1024]{0,1:T(8,128)(2,1)} %scatter_custom_fusion.1) | copy-start | bytes 1179652
  246.2 75.4 %copy-start.6 = (f32[192,11,128]{0,1,2:T(8,128)S(1)}, f32[192,11,128]{0,1,2:T(8,128)}, u32[]{:S(2)}) copy-start(f32[192,11,128]{0,1,2:T(8,128)} %fusion.10) | copy-start | bytes 3244036
  (72 other events, 225.2 us)
Sparse Core Ops, SparseCore 0:
  18.0 45.3 all-gather.2
  225.0 46.8 all-gather.4
  277.3 146.6 all-reduce.2
where the time goes:
time: 441 us; the launch traced here: 435 us
  other arithmetic  134 us (30%)
  waiting for transfers between devices  106 us (24%)
  local copies, waits for them, and re-layouts  77.1 us (17%)
  blocking collectives  69.4 us (16%)
  starting transfers between devices  18.7 us (4%)
  between operations  15.6 us (4%)
  matrix products  13.5 us (3%)
    psum x1, waiting for transfers between devices, on_device(): lax.psum((kernel_local, grad_expand, grad_project), ('lon', 'lat'))  87.9 us
    add x1, other arithmetic, on_device(): adjoint + depth_kernel[:, 7 * row_off + col_off][:, None, None] * padded[...  75.6 us
    psum x1, blocking collectives, on_device(): lax.psum((kernel_local, grad_expand, grad_project), ('lon', 'lat'))  69.4 us
    reduce_sum x3, other arithmetic, on_device(): jnp.sum(ext_f32[:, row_off:row_off + lat_cells, col_off:col_off + lon_cel...  12.5 us
    unnamed x198, local copies, waits for them, and re-layouts  11.6 us
    all_gather x1, waiting for transfers between devices, on_device(): gathered = lax.all_gather(top_rows, 'lon', axis=2, tiled=True)  10.5 us
    ppermute x4, starting transfers between devices, padded_2(): before = lax.ppermute(last, axis, up)  9.68 us
  transfers between devices with their start and end apart: 11, of which 5 were waited for; matrix products, arithmetic and copies ran while one was open for 22% of the time, Pallas kernels for 0%

commit v1 on v0

v1 whole, which is shorter than its diff:
```python
import functools

import jax
import jax.numpy as jnp
from jax import lax
from jax.experimental import pallas as pl
from jax.experimental.pallas import tpu as pltpu
from jax.sharding import PartitionSpec as P

MESH = pl.DeviceIdType.MESH
F32 = jnp.float32
BF16 = jnp.bfloat16
ROOT_HALF = 0.7071067811865476
ROOT_TWOPI_INV = 0.3989422804014327

C = 192
HID = 768
TY = 8
TX = 128
EXT = TY + 6
CELLS = TY * TX
TAPS = 49
GROUPS = 4
GC = C // GROUPS
WROWS = 2 * C * HID // 128
KROWS = 256
PIECE = 48


def dot_nn(a, b):
    return jnp.dot(a, b, preferred_element_type=F32)


def dot_nt(a, b):
    return lax.dot_general(a, b, (((1,), (1,)), ((), ())), preferred_element_type=F32)


def wait_bytes(ref, sem):
    pltpu.make_async_copy(ref, ref, sem).wait()


def column(row_ref):
    n = row_ref.shape[1]
    eye = lax.broadcasted_iota(jnp.int32, (n, n), 0) == lax.broadcasted_iota(
        jnp.int32, (n, n), 1
    )
    return jnp.sum(jnp.where(eye, row_ref[...], 0.0), axis=1, keepdims=True)


def pack_edges(rows, west, east):
    lane = lax.broadcasted_iota(jnp.int32, (GC, 128), 1)
    w = jnp.zeros((GC, 128), F32)
    e = jnp.zeros((GC, 128), F32)
    for q in range(GROUPS):
        for j in range(TY):
            at = 32 * q + 4 * j
            x = rows[3 + j, q * GC : (q + 1) * GC, :]
            slot = (lane >= at) & (lane < at + 4)
            w = jnp.where(slot, pltpu.roll(x, at, 1) if at else x, w)
            e = jnp.where(slot, pltpu.roll(x, (at + 4) % 128, 1), e)
    west[...] = w.astype(BF16)
    east[...] = e.astype(BF16)


def unpack_edges(edges, halo):
    lane = lax.broadcasted_iota(jnp.int32, (GC, 128), 1)
    for part, (r0, r1, j0) in enumerate(((0, 3, 5), (3, 11, 0), (11, 14, 0))):
        left = edges[part].astype(F32)
        right = edges[3 + part].astype(F32)
        for r in range(r0, r1):
            j = r - r0 + j0
            for q in range(GROUPS):
                at = 32 * q + 4 * j
                lf = pltpu.roll(left, (124 - at) % 128, 1) if at != 124 else left
                rt = pltpu.roll(right, (128 - at) % 128, 1) if at else right
                halo[r, q * GC : (q + 1) * GC, :] = jnp.where(lane < 64, rt, lf)


def shifted_rows(rows, halo, c0, r0, r1, d, lane):
    sh = d - 3
    x = rows[r0:r1, pl.ds(c0, 8), :]
    if sh == 0:
        return x
    h = halo[r0:r1, pl.ds(c0, 8), :]
    m = (lane < sh) if sh > 0 else (lane >= 128 + sh)
    return pltpu.roll(jnp.where(m, h, x), (-sh) % 128, 2)


def conv_tile(rows, halo, dk, c0, reverse):
    lane = lax.broadcasted_iota(jnp.int32, (EXT, 8, 128), 2)
    kv = dk[pl.ds(c0, 8), :]
    acc = jnp.zeros((TY, 8, 128), F32)
    for d in range(7):
        x = shifted_rows(rows, halo, c0, 0, EXT, d, lane)
        for a in range(7):
            t = 7 * a + d
            if reverse:
                t = TAPS - 1 - t
            acc = acc + kv[:, t : t + 1][None] * x[a : a + TY]
    return acc


def block_kernel(
    bands,
    sectors,
    state,
    cot,
    dk,
    gain,
    lscale,
    w_expand,
    w_project,
    cells,
    counts,
    partner,
    out_rows,
    grad_rows,
    sums_out,
    nat,
    ext,
    halo,
    gext,
    ghalo,
    cotr,
    conv,
    upstream,
    scaled,
    hidden,
    gradpre,
    wexpt,
    wprojt,
    wet,
    dkp,
    gk,
    sendrows,
    sendedge,
    recvrows,
    recvedge,
    gsendrows,
    gsendedge,
    grecvrows,
    grecvedge,
    foldrecv,
    foldsend2,
    foldrecv2,
    onehot,
    part,
    partrecv,
    total,
    totalrecv,
    full,
    final,
    sems,
):
    wch = WROWS // bands
    kch = KROWS // bands
    chunk = wch + kch
    piece = totalrecv.shape[1]
    lat = lax.axis_index("lat")
    lon = lax.axis_index("lon")
    is_south = lat == 0
    is_north = lat == bands - 1

    def peer(dlat, dlon):
        return {
            "lat": lax.rem(lat + (dlat + bands), bands),
            "lon": lax.rem(lon + (dlon + sectors), sectors),
        }

    def send(src, dst, s, device):
        cp = pltpu.make_async_remote_copy(
            src_ref=src,
            dst_ref=dst,
            send_sem=sems.at[2 * s],
            recv_sem=sems.at[2 * s + 1],
            device_id=device,
            device_id_type=MESH,
        )
        cp.start()

    barrier = pltpu.get_barrier_semaphore()
    peers = [(o, 0) for o in range(1, bands)] + [(0, o) for o in range(1, sectors)]
    peers += [(1, 1), (1, -1), (-1, 1), (-1, -1)]
    for dlat, dlon in peers:
        pl.semaphore_signal(barrier, inc=1, device_id=peer(dlat, dlon), device_id_type=MESH)

    nat[...] = state[...].astype(F32)
    for j in range(TY):
        ext[3 + j] = nat[pl.ds(j, C, stride=TY), :]
    for k, j in enumerate((0, 1, 2, 5, 6, 7)):
        sendrows[k * C : (k + 1) * C, :] = ext[3 + j].astype(BF16)
    pack_edges(ext, sendedge.at[0], sendedge.at[1])

    pl.semaphore_wait(barrier, len(peers))

    def exchange(rows_s, edge_s, rows_r, edge_r, s):
        send(rows_s.at[pl.ds(0, 3 * C)], rows_r.at[pl.ds(3 * C, 3 * C)], s, peer(-1, 0))
        send(rows_s.at[pl.ds(3 * C, 3 * C)], rows_r.at[pl.ds(0, 3 * C)], s, peer(1, 0))
        for n, dlat in enumerate((1, 0, -1)):
            send(edge_s.at[1], edge_r.at[n], s + 1, peer(dlat, 1))
            send(edge_s.at[0], edge_r.at[3 + n], s + 1, peer(dlat, -1))

    @pl.when(is_north)
    def _():
        for o in range(1, sectors):
            send(
                sendrows.at[pl.ds(3 * C, 3 * C)],
                foldrecv.at[pl.ds(lon * (3 * C), 3 * C)],
                2,
                peer(0, o),
            )

    exchange(sendrows, sendedge, recvrows, recvedge, 0)

    seg = lax.broadcasted_iota(jnp.int32, (1, CELLS), 1)
    capacity = CELLS // bands
    filled = jnp.zeros((1, CELLS), jnp.int32)
    for p in range(bands):
        filled = jnp.where(seg // capacity == p, counts[0, p], filled)
    live = (seg % capacity) < filled
    row_of = jnp.right_shift(cells[...], 7)
    col_of = jnp.bitwise_and(cells[...], 127)
    in_row = (lax.broadcasted_iota(jnp.int32, (TY, CELLS), 0) == row_of) & live
    in_col = lax.broadcasted_iota(jnp.int32, (TX, CELLS), 0) == col_of
    wet[...] = dot_nt(
        jnp.where(in_row, 1.0, 0.0).astype(BF16), jnp.where(in_col, 1.0, 0.0).astype(BF16)
    )
    gain_c = column(gain)
    scale_c = column(lscale)
    nat[...] = cot[...].astype(F32)
    for j in range(TY):
        x = nat[pl.ds(j, C, stride=TY), :]
        cotr[j] = x
        upstream[:, j * TX : (j + 1) * TX] = (wet[j : j + 1, :] * scale_c * x).astype(BF16)
    wexpt[...] = w_expand[...].astype(F32).T.astype(BF16)
    wprojt[...] = w_project[...].astype(F32).T.astype(BF16)
    dkp[...] = jnp.zeros((C, 128), F32)
    dkp[:, :TAPS] = dk[...]
    gk[C:, :] = jnp.zeros((KROWS - C, 128), F32)

    left = lax.rem(lon + sectors - 1, sectors)
    right = lax.rem(lon + 1, sectors)

    @pl.when(is_north)
    def _():
        mine = partner[pl.ds(lon, 1), :]
        lane = lax.broadcasted_iota(jnp.int32, (1, TX), 1)
        near = jnp.where(lane < 64, partner[pl.ds(right, 1), :], partner[pl.ds(left, 1), :])
        wanted = jnp.concatenate([mine, near], axis=1)
        for s in range(sectors):
            col = lax.broadcasted_iota(jnp.int32, (TX, 2 * TX), 0) + s * TX
            onehot[s] = jnp.where(col == wanted, 1.0, 0.0).astype(BF16)
        foldrecv[pl.ds(lon * (3 * C), 3 * C), :] = sendrows[3 * C :, :]

    def fill_halo(rows_r, edge_r, rows, hal, s):
        wait_bytes(rows_r, sems.at[2 * s + 1])
        wait_bytes(edge_r, sems.at[2 * s + 3])
        for k in range(3):
            rows[k] = jnp.where(is_south, 0.0, rows_r[k * C : (k + 1) * C, :].astype(F32))
            rows[11 + k] = jnp.where(
                is_north, 0.0, rows_r[(3 + k) * C : (4 + k) * C, :].astype(F32)
            )
        unpack_edges(edge_r, hal)

        @pl.when(is_south)
        def _():
            hal[0:3] = jnp.zeros((3, C, 128), F32)

        @pl.when(is_north)
        def _():
            hal[11:14] = jnp.zeros((3, C, 128), F32)

    fill_halo(recvrows, recvedge, ext, halo, 0)

    @pl.when(is_north)
    def _():
        wait_bytes(foldrecv.at[pl.ds(0, (sectors - 1) * 3 * C)], sems.at[5])
        for k in range(3):
            acc = jnp.zeros((C, 2 * TX), F32)
            for s in range(sectors):
                base = s * 3 * C + (2 - k) * C
                acc = acc + dot_nn(foldrecv[base : base + C, :], onehot[s])
            ext[11 + k] = acc[:, :TX]
            halo[11 + k] = acc[:, TX:]

    def conv_body(ct, carry):
        c0 = pl.multiple_of(ct * 8, 8)
        acc = conv_tile(ext, halo, dkp, c0, False)
        conv[:, pl.ds(c0, 8), :] = acc.astype(BF16).astype(F32)
        return carry

    lax.fori_loop(0, C // 8, conv_body, 0)

    def mlp_body(m, carry):
        at = pl.ds(pl.multiple_of(m * 256, 256), 256)
        v = jnp.concatenate([conv[2 * m], conv[2 * m + 1]], axis=1)
        center = v - jnp.mean(v, axis=0, keepdims=True)
        variance = jnp.mean(center * center, axis=0, keepdims=True)
        inv_std = lax.rsqrt(variance + 1e-06)
        normed = center * inv_std
        sc = (normed * gain_c).astype(BF16)
        scaled[:, at] = sc
        up = upstream[:, at]
        for h in range(0, HID, 256):
            pre = dot_nn(wexpt[h : h + 256, :], sc)
            gh = dot_nn(w_project[h : h + 256, :], up)
            half = 0.5 * (1.0 + lax.erf(pre * ROOT_HALF))
            hidden[h : h + 256, at] = (pre * half).astype(BF16)
            slope = half + pre * jnp.exp(-0.5 * pre * pre) * ROOT_TWOPI_INV
            gradpre[h : h + 256, at] = (gh * slope).astype(BF16)
        branch = dot_nn(wprojt[...], hidden[:, at]).astype(BF16).astype(F32)
        gs = dot_nn(w_expand[...], gradpre[:, at]) * gain_c
        gr = inv_std * (
            gs
            - jnp.mean(gs, axis=0, keepdims=True)
            - normed * jnp.mean(gs * normed, axis=0, keepdims=True)
        )
        gr = gr.astype(BF16).astype(F32)
        for n in range(2):
            half_at = slice(n * TX, (n + 1) * TX)
            j = 2 * m + n
            b = wet[pl.ds(j, 1), :] * scale_c * branch[:, half_at]
            out_rows[j] = (ext[3 + j] + b).astype(BF16)
            gext[3 + j] = gr[:, half_at]
        return carry

    lax.fori_loop(0, TY // 2, mlp_body, 0)

    for k, j in enumerate((0, 1, 2, 5, 6, 7)):
        gsendrows[k * C : (k + 1) * C, :] = gext[3 + j].astype(BF16)
    pack_edges(gext, gsendedge.at[0], gsendedge.at[1])
    exchange(gsendrows, gsendedge, grecvrows, grecvedge, 3)

    def gk_body(ct, carry):
        c0 = pl.multiple_of(ct * 8, 8)
        lane = lax.broadcasted_iota(jnp.int32, (EXT, 8, 128), 2)
        g = gext[3 : 3 + TY, pl.ds(c0, 8), :]
        res = jnp.zeros((8, 128), F32)
        for d in range(7):
            x = shifted_rows(ext, halo, c0, 0, EXT, d, lane)
            for a in range(7):
                s = jnp.sum(x[a : a + TY] * g, axis=0)
                res = jnp.where(lane[0] == 7 * a + d, jnp.sum(s, axis=1, keepdims=True), res)
        gk[pl.ds(c0, 8), :] = res
        return carry

    lax.fori_loop(0, C // 8, gk_body, 0)

    def put(w, value):
        part[(w // wch) * chunk + w % wch : (w // wch) * chunk + w % wch + PIECE, :] = value

    ge = dot_nt(scaled[...], gradpre[...])
    for b in range(HID // 128):
        for r in range(0, C, PIECE):
            put(b * C + r, ge[r : r + PIECE, b * 128 : (b + 1) * 128].astype(BF16))
    gp = dot_nt(hidden[...], upstream[...])
    base = C * HID // 128
    for r in range(0, HID, PIECE):
        put(base + r, gp[r : r + PIECE, :128].astype(BF16))
    hh = HID // 2
    for r in range(0, hh, PIECE):
        value = jnp.concatenate(
            [gp[r : r + PIECE, 128:], gp[hh + r : hh + r + PIECE, 128:]], axis=1
        )
        put(base + HID + r, value.astype(BF16))
    for p in range(bands):
        value = gk[p * kch : (p + 1) * kch, :].astype(BF16)
        part[p * chunk + wch : (p + 1) * chunk, :] = value

    for o in range(1, bands):
        to = peer(o, 0)
        send(part.at[pl.ds(to["lat"] * chunk, chunk)], partrecv.at[o - 1], 5, to)

    fill_halo(grecvrows, grecvedge, gext, ghalo, 3)

    @pl.when(is_north)
    def _():
        def fold_body(ct, carry):
            c0 = pl.multiple_of(ct * 8, 8)
            lane = lax.broadcasted_iota(jnp.int32, (3, 8, 128), 2)
            kv = dkp[pl.ds(c0, 8), :]
            acc = [jnp.zeros((8, 128), F32) for _ in range(3)]
            for d in range(7):
                x = shifted_rows(gext, ghalo, c0, 8, 11, d, lane)
                for k in range(3):
                    for a in range(3 - k):
                        t = TAPS - 1 - (7 * a + d)
                        acc[k] = acc[k] + kv[:, t : t + 1] * x[k + a]
            for k in range(3):
                ghalo[11 + k, pl.ds(c0, 8), :] = acc[k]
            return carry

        lax.fori_loop(0, C // 8, fold_body, 0)
        for k in range(3):
            foldsend2[k * C : (k + 1) * C, :] = ghalo[11 + k].astype(BF16)
            ghalo[11 + k] = jnp.zeros((C, 128), F32)
        for o in range(1, sectors):
            send(
                foldsend2,
                foldrecv2.at[pl.ds(lon * (3 * C), 3 * C)],
                6,
                peer(0, o),
            )

    def adj_body(ct, carry):
        c0 = pl.multiple_of(ct * 8, 8)
        acc = conv_tile(gext, ghalo, dkp, c0, True)
        conv[:, pl.ds(c0, 8), :] = acc + cotr[:, pl.ds(c0, 8), :]
        return carry

    lax.fori_loop(0, C // 8, adj_body, 0)

    wait_bytes(partrecv, sems.at[11])
    own = part[pl.ds(pl.multiple_of(lat * chunk, 16), chunk), :].astype(F32)
    for o in range(1, bands):
        own = own + partrecv[o - 1].astype(F32)
    total[0:chunk, :] = own
    if total.shape[0] > chunk:
        total[chunk:, :] = jnp.zeros((total.shape[0] - chunk, 128), F32)
    for o in range(1, sectors):
        to = peer(0, o)
        send(total.at[pl.ds(to["lon"] * piece, piece)], totalrecv.at[o - 1], 7, to)
    mine = pl.ds(pl.multiple_of(lon * piece, 8), piece)
    acc = total[mine, :]
    wait_bytes(totalrecv, sems.at[15])
    for o in range(1, sectors):
        acc = acc + totalrecv[o - 1]
    full[mine, :] = acc
    for o in range(1, sectors):
        send(full.at[pl.ds(lon * piece, piece)], full.at[pl.ds(lon * piece, piece)], 8, peer(0, o))
    wait_bytes(full.at[pl.ds(0, (sectors - 1) * piece)], sems.at[17])
    mine = pl.ds(pl.multiple_of(lat * chunk, 16), chunk)
    final[mine, :] = full[0:chunk, :].astype(BF16)
    for o in range(1, bands):
        send(final.at[pl.ds(lat * chunk, chunk)], final.at[pl.ds(lat * chunk, chunk)], 9, peer(o, 0))

    @pl.when(is_north)
    def _():
        foldrecv2[pl.ds(lon * (3 * C), 3 * C), :] = foldsend2[...]
        wait_bytes(foldrecv2.at[pl.ds(0, (sectors - 1) * 3 * C)], sems.at[13])
        col = lax.broadcasted_iota(jnp.int32, (TX, TX), 0) + lon * TX
        for k in range(3):
            acc = jnp.zeros((C, TX), F32)
            for s in range(sectors):
                here = jnp.where(partner[s : s + 1, :] == col, 1.0, 0.0).astype(BF16)
                base = s * 3 * C + k * C
                acc = acc + dot_nt(foldrecv2[base : base + C, :], here)
            conv[7 - k] = conv[7 - k] + acc

    for j in range(TY):
        grad_rows[j] = conv[j].astype(BF16)

    wait_bytes(final.at[pl.ds(0, (bands - 1) * chunk)], sems.at[19])
    sums_out[...] = final[...]

    wait_bytes(recvrows, sems.at[0])
    wait_bytes(recvedge, sems.at[2])
    wait_bytes(grecvrows, sems.at[6])
    wait_bytes(grecvedge, sems.at[8])
    wait_bytes(partrecv, sems.at[10])
    wait_bytes(totalrecv, sems.at[14])
    wait_bytes(totalrecv, sems.at[16])
    wait_bytes(final.at[pl.ds(0, (bands - 1) * chunk)], sems.at[18])

    @pl.when(is_north)
    def _():
        wait_bytes(foldrecv.at[pl.ds(0, (sectors - 1) * 3 * C)], sems.at[4])
        wait_bytes(foldrecv2.at[pl.ds(0, (sectors - 1) * 3 * C)], sems.at[12])


def finish_kernel(
    bands, out_rows, grad_rows, sums, out_field, grad_field, gk, ge, gp, nat
):
    wch = WROWS // bands
    kch = KROWS // bands
    chunk = wch + kch
    for src, dst in ((out_rows, out_field), (grad_rows, grad_field)):
        for j in range(TY):
            nat[pl.ds(j, C, stride=TY), :] = src[j].astype(F32)
        dst[...] = nat[...].astype(BF16)

    def get(w):
        at = (w // wch) * chunk + w % wch
        return sums[at : at + PIECE, :].astype(F32)

    for b in range(HID // 128):
        for r in range(0, C, PIECE):
            ge[r : r + PIECE, b * 128 : (b + 1) * 128] = get(b * C + r)
    base = C * HID // 128
    hh = HID // 2
    for r in range(0, HID, PIECE):
        gp[r : r + PIECE, :128] = get(base + r)
    for r in range(0, hh, PIECE):
        x = get(base + HID + r)
        gp[r : r + PIECE, 128:] = x[:, : C - 128]
        gp[hh + r : hh + r + PIECE, 128:] = x[:, C - 128 :]
    for r in range(0, C, 16):
        at = (r // kch) * chunk + wch + r % kch
        gk[r : r + 16, :] = sums[at : at + 16, :TAPS].astype(F32)


def on_device(
    bands,
    sectors,
    state_field,
    depth_kernel,
    norm_gain,
    w_expand,
    w_project,
    layer_scale,
    cotangent,
    send_cells,
    send_count,
    fold_partner,
):
    chunk = (WROWS + KROWS) // bands
    piece = -(-chunk // (8 * sectors)) * 8
    vmem = pl.BlockSpec(memory_space=pltpu.VMEM)
    smem = pl.BlockSpec(memory_space=pltpu.SMEM)
    sds = jax.ShapeDtypeStruct
    rows3 = pltpu.VMEM((6 * C, 128), BF16)
    edge = pltpu.VMEM((6, GC, 128), BF16)
    fold = pltpu.VMEM((sectors * 3 * C, 128), BF16)
    scratch = dict(
        nat=pltpu.VMEM((C * TY, 128), F32),
        ext=pltpu.VMEM((EXT, C, 128), F32),
        halo=pltpu.VMEM((EXT, C, 128), F32),
        gext=pltpu.VMEM((EXT, C, 128), F32),
        ghalo=pltpu.VMEM((EXT, C, 128), F32),
        cotr=pltpu.VMEM((TY, C, 128), F32),
        conv=pltpu.VMEM((TY, C, 128), F32),
        upstream=pltpu.VMEM((C, CELLS), BF16),
        scaled=pltpu.VMEM((C, CELLS), BF16),
        hidden=pltpu.VMEM((HID, CELLS), BF16),
        gradpre=pltpu.VMEM((HID, CELLS), BF16),
        wexpt=pltpu.VMEM((HID, C), BF16),
        wprojt=pltpu.VMEM((C, HID), BF16),
        wet=pltpu.VMEM((TY, TX), F32),
        dkp=pltpu.VMEM((C, 128), F32),
        gk=pltpu.VMEM((KROWS, 128), F32),
        sendrows=rows3,
        sendedge=pltpu.VMEM((2, GC, 128), BF16),
        recvrows=rows3,
        recvedge=edge,
        gsendrows=rows3,
        gsendedge=pltpu.VMEM((2, GC, 128), BF16),
        grecvrows=rows3,
        grecvedge=edge,
        foldrecv=fold,
        foldsend2=pltpu.VMEM((3 * C, 128), BF16),
        foldrecv2=fold,
        onehot=pltpu.VMEM((sectors, TX, 2 * TX), BF16),
        part=pltpu.VMEM((bands * chunk, 128), BF16),
        partrecv=pltpu.VMEM((bands - 1, chunk, 128), BF16),
        total=pltpu.VMEM((sectors * piece, 128), F32),
        totalrecv=pltpu.VMEM((sectors - 1, piece, 128), F32),
        full=pltpu.VMEM((sectors * piece, 128), F32),
        final=pltpu.VMEM((bands * chunk, 128), BF16),
        sems=pltpu.SemaphoreType.DMA((20,)),
    )
    out_rows, grad_rows, sums = pl.pallas_call(
        functools.partial(block_kernel, bands, sectors),
        out_shape=(
            sds((TY, C, 128), BF16),
            sds((TY, C, 128), BF16),
            sds((bands * chunk, 128), BF16),
        ),
        in_specs=[vmem] * 8 + [smem] + [vmem],
        out_specs=(vmem, vmem, vmem),
        scratch_shapes=list(scratch.values()),
        compiler_params=pltpu.CompilerParams(
            collective_id=0, has_side_effects=True, vmem_limit_bytes=48 * 2**20
        ),
        name="block",
    )(
        state_field.reshape(C * TY, TX),
        cotangent.reshape(C * TY, TX),
        depth_kernel,
        norm_gain.reshape(1, C),
        layer_scale.reshape(1, C),
        w_expand,
        w_project,
        send_cells,
        send_count,
        fold_partner.reshape(sectors, TX),
    )
    out_field, grad_field, gk, ge, gp = pl.pallas_call(
        functools.partial(finish_kernel, bands),
        out_shape=(
            sds((C * TY, TX), BF16),
            sds((C * TY, TX), BF16),
            sds((C, TAPS), F32),
            sds((C, HID), F32),
            sds((HID, C), F32),
        ),
        in_specs=[vmem] * 3,
        out_specs=(vmem,) * 5,
        scratch_shapes=[pltpu.VMEM((C * TY, 128), F32)],
        compiler_params=pltpu.CompilerParams(vmem_limit_bytes=32 * 2**20),
        name="finish",
    )(out_rows, grad_rows, sums)
    return (
        out_field.reshape(C, TY, TX),
        grad_field.reshape(C, TY, TX),
        gk,
        ge,
        gp,
    )


def solution(mesh):
    return jax.shard_map(
        functools.partial(on_device, mesh.shape["lat"], mesh.shape["lon"]),
        mesh=mesh,
        in_specs=(
            P(None, "lat", "lon"),
            P(),
            P(),
            P(),
            P(),
            P(),
            P(None, "lat", "lon"),
            P("lat", "lon"),
            P("lat", "lon"),
            P(),
        ),
        out_specs=(P(None, "lat", "lon"), P(None, "lat", "lon"), P(), P(), P()),
        check_vma=False,
    )
```

time: 441 us -> 78.9 us (0.18); the launches traced: 435 us -> 78.7 us
  other arithmetic: 134 us -> 0 us
  waiting for transfers between devices: 106 us -> 0 us
  Pallas kernels: 0 us -> 73 us
  local copies, waits for them, and re-layouts: 77.1 us -> 4.92 us
  blocking collectives: 69.4 us -> 0 us
  starting transfers between devices: 18.7 us -> 0 us
  between operations: 15.6 us -> 0.76 us
  matrix products: 13.5 us -> 0 us
    psum x1 -> x0, waiting for transfers between devices: 87.9 us -> none  [on_device(): lax.psum((kernel_local, grad_expand, grad_project), ('lon', 'lat'))]
    add x3 -> x0, other arithmetic: 77 us -> none  [the longest x1 75.6 us: on_device(): adjoint + depth_kernel[:, 7 * row_off + col_off][:, None, None] * padded[...]
    pallas_call x0 -> x2, Pallas kernels: none -> 73 us  [the longest x1 71.5 us: on_device(): pl.pallas_call(functools.partial(block_kernel, bands, sectors), out_shape...]
    psum x1 -> x0, blocking collectives: 69.4 us -> none  [on_device(): lax.psum((kernel_local, grad_expand, grad_project), ('lon', 'lat'))]
    convert_element_type x7 -> x0, other arithmetic: 22.9 us -> none  [the longest x1 8.69 us: on_device(): convolved.astype(jnp.bfloat16).reshape(channels, lat_cells * lon_cells)]
    gather x9 -> x0, local copies, waits for them, and re-layouts: 21.1 us -> none  [the longest x2 7.7 us: on_device(): packed = jnp.take(rounded, cell_list, axis=1)]
    ppermute x8 -> x0, starting transfers between devices: 18.4 us -> none  [the longest x4 9.68 us: padded_2(): before = lax.ppermute(last, axis, up)]
    reduce_sum x6 -> x0, other arithmetic: 15.9 us -> none  [the longest x3 12.5 us: on_device(): jnp.sum(ext_f32[:, row_off:row_off + lat_cells, col_off:col_off + lon_cel...]
  transfers between devices with their start and end apart: 11 -> 0, of which waited for: 5 -> 0; matrix products, arithmetic and copies ran while one was open for 22% -> 0% of each run, Pallas kernels for 0% -> 0%
where the time goes in v1:
time: 78.9 us; the launch traced here: 78.7 us
  Pallas kernels  73 us (93%)
  local copies, waits for them, and re-layouts  4.92 us (6%)
    pallas_call x1, Pallas kernels, on_device(): pl.pallas_call(functools.partial(block_kernel, bands, sectors), out_shape...  71.5 us
    unnamed x20, local copies, waits for them, and re-layouts  4.92 us

profile of v1, /device:TPU:1, one launch (start us, length us, event | category | flops | bytes accessed | tf_op | source)
XLA Modules:
  0.0 78.7 jit_solution(14134508318047537664)
XLA Ops:
  0.6 0.0 copy-start
  0.6 0.0 copy-start.1
  0.7 1.0 %copy.15.dk = f32[192,49]{1,0:T(8,128)S(1)} copy(f32[192,49]{0,1:T(8,128)} %param.11) | data formatting | bytes 75264 | tf_op args[1]
  1.6 0.0 copy-start.3
  1.7 0.0 copy-start.4
  1.7 0.0 copy-start.5
  1.7 0.0 copy-start.6
  1.7 0.0 copy-start.7
  1.7 1.2 %copy.16.w_project = bf16[768,192]{1,0:T(8,128)(2,1)S(1)} copy(bf16[768,192]{0,1:T(8,128)(2,1)} %param.14) | data formatting | bytes 589824 | tf_op args[4]
  2.9 0.0 copy-done
  2.9 0.0 copy-done.1
  2.9 0.0 copy-done.3
  2.9 0.0 copy-done.4
  2.9 0.0 copy-done.5
  2.9 0.0 copy-done.6
  2.9 0.0 copy-done.7
  2.9 0.0 copy-start.2
  2.9 1.0 %copy-done.2 = bf16[192,768]{1,0:T(8,128)(2,1)S(1)} copy-done((bf16[192,768]{1,0:T(8,128)(2,1)S(1)}, bf16[192,768]{1,0:T(8,128)(2,1)}, u32[]{:S(2)}) %copy-start.2) | copy-done | bytes 294936
  3.9 71.5 %block.1 = (bf16[8,192,128]{2,1,0:T(8,128)(2,1)S(1)}, bf16[8,192,128]{2,1,0:T(8,128)(2,1)S(1)}, bf16[2560,128]{1,0:T(8,128)(2,1)S(1)}) custom-call(bf16[1536,128]{1,0:T(8,128)(2,1)S(1)} %bitcast.7, bf16[1536,128]{1,0:T(8,128)(2,1)S(1)} %bitcast.8, f32[192,49]{1,0:T(8,128)S(1)} %copy.15.dk, f32[1,192]{1,0:T(1,128)S(1)} %bitcast.10, f32[1,192]{1,0:T(1,128)S(1)} %bitcast.11, ...), custom_call_target="tpu_custom_call" | custom-call | tf_op jit(solution)/shard_map/block/pallas_call | solution.py:561
  75.4 1.5 %finish.1 = (bf16[1536,128]{1,0:T(8,128)(2,1)}, bf16[1536,128]{1,0:T(8,128)(2,1)}, f32[192,49]{1,0:T(8,128)S(1)}, f32[192,768]{1,0:T(8,128)}, f32[768,192]{1,0:T(8,128)S(1)}) custom-call(bf16[8,192,128]{2,1,0:T(8,128)(2,1)S(1)} %get-tuple-element.13.out_rows, bf16[8,192,128]{2,1,0:T(8,128)(2,1)S(1)} %get-tuple-element.14.grad_rows, ...), custom_call_target="tpu_custom_call" | custom-call | tf_op jit(solution)/shard_map/finish/pallas_call | solution.py:587
  76.9 0.7 copy.17
  77.6 1.1 %copy.18 = f32[768,192]{0,1:T(8,128)} copy(f32[768,192]{1,0:T(8,128)S(1)} %get-tuple-element.25) | data formatting | bytes 1179648
Async XLA Ops:
  0.6 2.2 %copy-start = (bf16[192,8,128]{2,1,0:T(8,128)(2,1)S(1)}, bf16[192,8,128]{2,1,0:T(8,128)(2,1)}, u32[]{:S(2)}) copy-start(bf16[192,8,128]{2,1,0:T(8,128)(2,1)} %param.10) | copy-start | bytes 1179652
  0.6 2.2 %copy-start.1 = (bf16[192,8,128]{2,1,0:T(8,128)(2,1)S(1)}, bf16[192,8,128]{2,1,0:T(8,128)(2,1)}, u32[]{:S(2)}) copy-start(bf16[192,8,128]{2,1,0:T(8,128)(2,1)} %param.16) | copy-start | bytes 1179652
  1.6 1.2 %copy-start.3 = (s32[1,1024]{1,0:T(1,128)S(1)}, s32[1,1024]{1,0:T(1,128)}, u32[]{:S(2)}) copy-start(s32[1,1024]{1,0:T(1,128)} %cells.1) | copy-start | bytes 12292
  1.7 1.2 %copy-start.4 = (s32[1024]{0:T(1024)S(1)}, s32[1024]{0:T(1024)}, u32[]{:S(2)}) copy-start(s32[1024]{0:T(1024)} %param.19) | copy-start | bytes 12292
  1.7 1.2 %copy-start.5 = (f32[192]{0:T(256)S(1)}, f32[192]{0:T(256)}, u32[]{:S(2)}) copy-start(f32[192]{0:T(256)} %param.12) | copy-start | bytes 2308
  1.7 1.2 %copy-start.6 = (f32[192]{0:T(256)S(1)}, f32[192]{0:T(256)}, u32[]{:S(2)}) copy-start(f32[192]{0:T(256)} %param.15) | copy-start | bytes 2308
  1.7 1.2 %copy-start.7 = (s32[1,16]{1,0:T(1,128)S(1)}, s32[1,16]{1,0:T(1,128)}, u32[]{:S(2)}) copy-start(s32[1,16]{1,0:T(1,128)} %counts.1) | copy-start | bytes 196
  2.9 1.0 %copy-start.2 = (bf16[192,768]{1,0:T(8,128)(2,1)S(1)}, bf16[192,768]{1,0:T(8,128)(2,1)}, u32[]{:S(2)}) copy-start(bf16[192,768]{1,0:T(8,128)(2,1)} %w_expand.1) | copy-start | bytes 884740

commit v2 on v1

v2 whole, which is shorter than its diff:
```python
import functools

import jax
import jax.numpy as jnp
from jax import lax
from jax.experimental import pallas as pl
from jax.experimental.pallas import tpu as pltpu
from jax.sharding import PartitionSpec as P

MESH = pl.DeviceIdType.MESH
F32 = jnp.float32
BF16 = jnp.bfloat16
ROOT_HALF = 0.7071067811865476
ROOT_TWOPI_INV = 0.3989422804014327

C = 192
HID = 768
TY = 8
TX = 128
EXT = TY + 6
CELLS = TY * TX
TAPS = 49
GROUPS = 4
GC = C // GROUPS
WROWS = 2 * C * HID // 128
PIECE = 96


def dot_nn(a, b):
    return jnp.dot(a, b, preferred_element_type=F32)


def dot_nt(a, b):
    return lax.dot_general(a, b, (((1,), (1,)), ((), ())), preferred_element_type=F32)


def wait_bytes(ref, sem):
    pltpu.make_async_copy(ref, ref, sem).wait()


def column(row_ref):
    n = row_ref.shape[1]
    eye = lax.broadcasted_iota(jnp.int32, (n, n), 0) == lax.broadcasted_iota(
        jnp.int32, (n, n), 1
    )
    return jnp.sum(jnp.where(eye, row_ref[...], 0.0), axis=1, keepdims=True)


def slot_lanes(shape, base, n):
    lane = lax.broadcasted_iota(jnp.int32, shape, len(shape) - 1)
    return (lane >= base) & (lane < base + n)


def turn(x, shift):
    shift %= 128
    return pltpu.roll(x, shift, x.ndim - 1) if shift else x


def pack_edges(rows, packed):
    shape = (GC, 128)
    for q in range(GROUPS):
        at = slice(q * GC, (q + 1) * GC)
        p = jnp.zeros(shape, F32)
        for j in range(TY):
            x = rows[3 + j, at, :]
            p = jnp.where(slot_lanes(shape, 4 * j, 3), turn(x, 4 * j), p)
            p = jnp.where(slot_lanes(shape, 64 + 4 * j, 3), turn(x, 64 + 4 * j - 125), p)
        packed[at, :] = p


def edge_messages(packed, west, east):
    shape = (GC, 128)
    w = packed[0:GC, :]
    e = turn(w, 64)
    for q in range(1, GROUPS):
        x = packed[q * GC : (q + 1) * GC, :]
        here = slot_lanes(shape, 32 * q, 32)
        w = jnp.where(here, turn(x, 32 * q), w)
        e = jnp.where(here, turn(x, 32 * q - 64), e)
    west[...] = w.astype(BF16)
    east[...] = e.astype(BF16)


def unpack_edges(msgs, edge, is_south, is_north):
    shape = (GC, 128)
    lane = lax.broadcasted_iota(jnp.int32, shape, 1)
    within = jnp.bitwise_and(lane, 63)
    dead = (is_south & (within < 12)) | (is_north & (within >= 44))
    values = [msgs[n].astype(F32) for n in range(6)]
    for q in range(GROUPS):
        p = jnp.zeros(shape, F32)
        for side in range(2):
            for n, (at, width, j0) in enumerate(((0, 12, 5), (12, 32, 0), (44, 12, 0))):
                to = 64 * side + at
                x = turn(values[3 * side + n], to - 32 * q - 4 * j0)
                p = jnp.where(slot_lanes(shape, to, width), x, p)
        edge[q * GC : (q + 1) * GC, :] = jnp.where(dead, 0.0, p)


def shifted(x, d):
    sh = d - 3
    if sh == 0:
        return x
    lane = lax.broadcasted_iota(jnp.int32, x.shape, x.ndim - 1)
    x = jnp.where((lane >= sh) if sh > 0 else (lane < 128 + sh), x, 0.0)
    return turn(x, -sh)


def tap(a, d, reverse):
    t = 7 * a + d
    return TAPS - 1 - t if reverse else t


def conv_own(rows, kb, cs, reverse, acc):
    x = rows[3 : 3 + TY, cs, :]
    for d in range(7):
        y = shifted(x, d)
        for a in range(7):
            k = kb[tap(a, d, reverse), cs, :]
            for j in range(max(0, 3 - a), min(TY, 11 - a)):
                acc[j] = acc[j] + k * y[j + a - 3]
    return acc


def edge_terms(edge, cs):
    shape = (cs.size, 128)
    lane = lax.broadcasted_iota(jnp.int32, shape, 1)
    within = jnp.bitwise_and(lane, 3)
    left = lane < 64
    e = edge[cs, :]
    terms = [jnp.where(within < 3, e, 0.0)]
    for s in (1, 2):
        lf = jnp.where(left & (within <= 2 - s), turn(e, -s), 0.0)
        terms.append(
            jnp.where((lane >= 64) & (within >= s) & (within < 3), turn(e, s), lf)
        )
    return terms


def edge_sums(edge, kb, cs, reverse, depth):
    left = slot_lanes((cs.size, 128), 0, 64)
    terms = edge_terms(edge, cs)
    total = None
    for a in range(depth):
        y = None
        for s in range(3):
            lf = kb[tap(a, s, reverse), cs, :]
            rt = kb[tap(a, 6 - s, reverse), cs, :]
            k = jnp.where(left, lf, rt)
            y = k * terms[s] if y is None else y + k * terms[s]
        y = turn(y, -4 * a)
        total = y if total is None else total + y
    return total


def edge_row(total, j):
    west = jnp.where(slot_lanes(total.shape, 0, 3), turn(total, -4 * j), 0.0)
    return jnp.where(slot_lanes(total.shape, 125, 3), turn(total, 61 - 4 * j), west)


def conv_halo(rows, kb, cs, reverse, acc, south, north):
    if south:
        lo_rows = rows[0:3, cs, :]
    if north:
        hi_rows = rows[3 + TY :, cs, :]
    for d in range(7):
        if south:
            lo = shifted(lo_rows, d)
            for a in range(3):
                k = kb[tap(a, d, reverse), cs, :]
                for r in range(a, 3):
                    acc[r - a] = acc[r - a] + k * lo[r]
        if north:
            hi = shifted(hi_rows, d)
            for a in range(4, 7):
                k = kb[tap(a, d, reverse), cs, :]
                for r in range(0, a - 3):
                    acc[11 + r - a] = acc[11 + r - a] + k * hi[r]
    return acc


def conv_edge(edge, kb, cs, reverse, acc, first):
    total = edge_sums(edge, kb, cs, reverse, 7)
    for j in range(first, TY):
        acc[j] = acc[j] + edge_row(total, j)
    return acc


def block_kernel(
    bands,
    sectors,
    state,
    cot,
    dkt,
    gain,
    lscale,
    w_expand,
    wprojt,
    cells,
    counts,
    partner,
    out_rows,
    grad_rows,
    sums_out,
    nat,
    ext,
    gext,
    edge,
    gedge,
    packed,
    gpacked,
    cotr,
    conv,
    upstream,
    scaled,
    hidden,
    gradpre,
    wexpt,
    w_project,
    wet,
    kb,
    fedge,
    gk,
    sendrows,
    sendedge,
    recvrows,
    recvedge,
    gsendrows,
    gsendedge,
    grecvrows,
    grecvedge,
    foldrecv,
    foldrecv2,
    onehot,
    onehot2,
    part,
    partrecv,
    gkrecv,
    total,
    totalrecv,
    full,
    final,
    sems,
):
    wch = WROWS // sectors
    kch = C // sectors
    chunk = wch + kch
    fch = final.shape[0] // sectors
    piece = totalrecv.shape[1]
    lat = lax.axis_index("lat")
    lon = lax.axis_index("lon")
    is_south = lat == 0
    is_north = lat == bands - 1

    def peer(dlat, dlon):
        return {
            "lat": lax.rem(lat + (dlat + bands), bands),
            "lon": lax.rem(lon + (dlon + sectors), sectors),
        }

    def send(src, dst, s, device):
        cp = pltpu.make_async_remote_copy(
            src_ref=src,
            dst_ref=dst,
            send_sem=sems.at[2 * s],
            recv_sem=sems.at[2 * s + 1],
            device_id=device,
            device_id_type=MESH,
        )
        cp.start()

    barrier = pltpu.get_barrier_semaphore()
    peers = [(o, 0) for o in range(1, bands)] + [(0, o) for o in range(1, sectors)]
    peers += [(1, 1), (1, -1), (-1, 1), (-1, -1)]
    for dlat, dlon in peers:
        pl.semaphore_signal(barrier, inc=1, device_id=peer(dlat, dlon), device_id_type=MESH)

    nat[...] = state[...].astype(F32)
    for j in range(TY):
        ext[3 + j] = nat[pl.ds(j, C, stride=TY), :]
    for k, j in enumerate((0, 1, 2, 5, 6, 7)):
        sendrows[k * C : (k + 1) * C, :] = ext[3 + j].astype(BF16)
    pack_edges(ext, packed)
    edge_messages(packed, sendedge.at[0], sendedge.at[1])

    seg = lax.broadcasted_iota(jnp.int32, (1, CELLS), 1)
    capacity = CELLS // bands
    filled = jnp.zeros((1, CELLS), jnp.int32)
    for p in range(bands):
        filled = jnp.where(seg // capacity == p, counts[0, p], filled)
    live = (seg % capacity) < filled
    row_of = jnp.right_shift(cells[...], 7)
    col_of = jnp.bitwise_and(cells[...], 127)
    in_row = (lax.broadcasted_iota(jnp.int32, (TY, CELLS), 0) == row_of) & live
    in_col = lax.broadcasted_iota(jnp.int32, (TX, CELLS), 0) == col_of
    wet[...] = dot_nt(
        jnp.where(in_row, 1.0, 0.0).astype(BF16), jnp.where(in_col, 1.0, 0.0).astype(BF16)
    )
    dkp = jnp.concatenate([dkt[...], jnp.zeros((128 - TAPS, C), F32)], axis=0).T
    for t in range(TAPS):
        kb[t] = jnp.broadcast_to(dkp[:, t : t + 1], (C, 128))

    pl.semaphore_wait(barrier, len(peers))

    def exchange(rows_s, edge_s, rows_r, edge_r, s):
        for n, dlat in enumerate((1, 0, -1)):
            send(edge_s.at[1], edge_r.at[n], s + 1, peer(dlat, 1))
            send(edge_s.at[0], edge_r.at[3 + n], s + 1, peer(dlat, -1))
        send(rows_s.at[pl.ds(0, 3 * C)], rows_r.at[pl.ds(3 * C, 3 * C)], s, peer(-1, 0))
        send(rows_s.at[pl.ds(3 * C, 3 * C)], rows_r.at[pl.ds(0, 3 * C)], s, peer(1, 0))

    exchange(sendrows, sendedge, recvrows, recvedge, 0)

    @pl.when(is_north)
    def _():
        for o in range(1, sectors):
            send(
                sendrows.at[pl.ds(3 * C, 3 * C)],
                foldrecv.at[pl.ds(lon * (3 * C), 3 * C)],
                2,
                peer(0, o),
            )

    gain_c = column(gain)
    scale_c = column(lscale)
    nat[...] = cot[...].astype(F32)
    for j in range(TY):
        x = nat[pl.ds(j, C, stride=TY), :]
        cotr[j] = x
        upstream[:, j * TX : (j + 1) * TX] = (wet[j : j + 1, :] * scale_c * x).astype(BF16)
    wexpt[...] = w_expand[...].astype(F32).T.astype(BF16)
    w_project[...] = wprojt[...].astype(F32).T.astype(BF16)

    left = lax.rem(lon + sectors - 1, sectors)
    right = lax.rem(lon + 1, sectors)

    @pl.when(is_north)
    def _():
        mine = partner[:, pl.ds(pl.multiple_of(lon * TX, TX), TX)]
        from_left = partner[:, pl.ds(pl.multiple_of(left * TX, TX), TX)]
        from_right = partner[:, pl.ds(pl.multiple_of(right * TX, TX), TX)]
        near = jnp.zeros((1, TX), jnp.int32)
        for r in range(3 + TY, EXT):
            near = jnp.where(slot_lanes((1, TX), 4 * r, 3), turn(from_left, 4 * r - 125), near)
            near = jnp.where(slot_lanes((1, TX), 64 + 4 * r, 3), turn(from_right, 64 + 4 * r), near)
        wanted = jnp.concatenate([mine, near], axis=1)
        for s in range(sectors):
            col = lax.broadcasted_iota(jnp.int32, (TX, 2 * TX), 0) + s * TX
            onehot[s] = jnp.where(col == wanted, 1.0, 0.0).astype(BF16)
        col = lax.broadcasted_iota(jnp.int32, (TX, sectors * TX), 0) + lon * TX
        for b in range(7):
            beside = partner[...] if b == 3 else pltpu.roll(partner[...], (3 - b) % (sectors * TX), 1)
            onehot2[b * TX : (b + 1) * TX, :] = jnp.where(beside == col, 1.0, 0.0).astype(BF16)
        foldrecv[pl.ds(lon * (3 * C), 3 * C), :] = sendrows[3 * C :, :]

    def each_tile(body, height):
        def step(ct, carry):
            body(pl.ds(pl.multiple_of(ct * height, 8), height))
            return carry

        lax.fori_loop(0, C // height, step, 0)

    def own_body(cs):
        acc = conv_own(ext, kb, cs, False, [jnp.zeros((cs.size, 128), F32) for _ in range(TY)])
        for j in range(TY):
            conv[j, cs, :] = acc[j]

    each_tile(own_body, 16)

    def fill_halo(rows_r, edge_r, rows, edges, s):
        wait_bytes(rows_r, sems.at[2 * s + 1])
        wait_bytes(edge_r, sems.at[2 * s + 3])
        for k in range(3):
            rows[k] = jnp.where(is_south, 0.0, rows_r[k * C : (k + 1) * C, :].astype(F32))
            rows[11 + k] = jnp.where(
                is_north, 0.0, rows_r[(3 + k) * C : (4 + k) * C, :].astype(F32)
            )
        unpack_edges(edge_r, edges, is_south, is_north)

    fill_halo(recvrows, recvedge, ext, edge, 0)

    def south_body(cs):
        acc = [conv[j, cs, :] for j in range(TY)]
        acc = conv_edge(edge, kb, cs, False, acc, 0)
        acc = conv_halo(ext, kb, cs, False, acc, True, False)
        for j in range(TY):
            conv[j, cs, :] = acc[j]

    each_tile(south_body, 24)

    def mlp_body(m, carry):
        at = pl.ds(pl.multiple_of(m * 256, 256), 256)
        v = jnp.concatenate([conv[2 * m], conv[2 * m + 1]], axis=1).astype(BF16).astype(F32)
        center = v - jnp.mean(v, axis=0, keepdims=True)
        variance = jnp.mean(center * center, axis=0, keepdims=True)
        inv_std = lax.rsqrt(variance + 1e-06)
        normed = center * inv_std
        sc = (normed * gain_c).astype(BF16)
        scaled[:, at] = sc
        up = upstream[:, at]
        for h in range(0, HID, 256):
            pre = dot_nn(wexpt[h : h + 256, :], sc)
            gh = dot_nn(w_project[h : h + 256, :], up)
            half = 0.5 * (1.0 + lax.erf(pre * ROOT_HALF))
            hidden[h : h + 256, at] = (pre * half).astype(BF16)
            slope = half + pre * jnp.exp(-0.5 * pre * pre) * ROOT_TWOPI_INV
            gradpre[h : h + 256, at] = (gh * slope).astype(BF16)
        branch = dot_nn(wprojt[...], hidden[:, at]).astype(BF16).astype(F32)
        gs = dot_nn(w_expand[...], gradpre[:, at]) * gain_c
        gr = inv_std * (
            gs
            - jnp.mean(gs, axis=0, keepdims=True)
            - normed * jnp.mean(gs * normed, axis=0, keepdims=True)
        )
        gr = gr.astype(BF16).astype(F32)
        for n in range(2):
            half_at = slice(n * TX, (n + 1) * TX)
            j = 2 * m + n
            b = wet[pl.ds(j, 1), :] * scale_c * branch[:, half_at]
            out_rows[j] = (ext[3 + j] + b).astype(BF16)
            gext[3 + j] = gr[:, half_at]
        return carry

    lax.fori_loop(0, TY // 4, mlp_body, 0)

    @pl.when(is_north)
    def _():
        wait_bytes(foldrecv.at[pl.ds(0, (sectors - 1) * 3 * C)], sems.at[5])
        corners = jnp.zeros((C, TX), F32)
        for k in range(3):
            acc = jnp.zeros((C, 2 * TX), F32)
            for s in range(sectors):
                base = s * 3 * C + (2 - k) * C
                acc = acc + dot_nn(foldrecv[base : base + C, :], onehot[s])
            ext[11 + k] = acc[:, :TX]
            at = 4 * (11 + k)
            here = slot_lanes((C, TX), at, 3) | slot_lanes((C, TX), 64 + at, 3)
            corners = jnp.where(here, acc[:, TX:], corners)
        fedge[...] = corners
        edge[...] = edge[...] + corners

        def corner_body(cs):
            acc = [None] * 5 + [conv[j, cs, :] for j in range(5, TY)]
            acc = conv_edge(fedge, kb, cs, False, acc, 5)
            for j in range(5, TY):
                conv[j, cs, :] = acc[j]

        each_tile(corner_body, 48)

    def north_body(cs):
        acc = [None] * 5 + [conv[j, cs, :] for j in range(5, TY)]
        acc = conv_halo(ext, kb, cs, False, acc, False, True)
        for j in range(5, TY):
            conv[j, cs, :] = acc[j]

    each_tile(north_body, 24)
    lax.fori_loop(TY // 4, TY // 2, mlp_body, 0)

    ge = dot_nt(scaled[...], gradpre[...]).astype(BF16)
    gpt = dot_nt(upstream[...], hidden[...]).astype(BF16)
    blocks = HID // 128
    for b in range(blocks):
        part[b * C : (b + 1) * C, :] = ge[:, b * 128 : (b + 1) * 128]
        part[(blocks + b) * C : (blocks + b + 1) * C, :] = gpt[:, b * 128 : (b + 1) * 128]
    for o in range(1, sectors):
        to = peer(0, o)
        send(part.at[pl.ds(to["lon"] * wch, wch)], partrecv.at[o - 1], 5, to)

    for k, j in enumerate((0, 1, 2, 5, 6, 7)):
        gsendrows[k * C : (k + 1) * C, :] = gext[3 + j].astype(BF16)
    pack_edges(gext, gpacked)
    edge_messages(gpacked, gsendedge.at[0], gsendedge.at[1])
    def gk_body(cs):
        lane = lax.broadcasted_iota(jnp.int32, (cs.size, 128), 1)
        x = ext[:, cs, :]
        g = gext[3 : 3 + TY, cs, :]
        terms = edge_terms(edge, cs)
        gp = gpacked[cs, :]
        beside = [turn(gp, 4 * a) for a in range(7)]
        res = jnp.zeros((cs.size, 128), F32)
        for d in range(7):
            y = shifted(g, 6 - d)
            for a in range(7):
                v = jnp.sum(x[a : a + TY] * y, axis=0)
                if d < 3:
                    v = v + jnp.where(lane < 64, terms[d] * beside[a], 0.0)
                if d > 3:
                    v = v + jnp.where(lane >= 64, terms[6 - d] * beside[a], 0.0)
                res = jnp.where(lane == 7 * a + d, jnp.sum(v, axis=1, keepdims=True), res)
        gk[cs, :] = res

    each_tile(gk_body, 16)
    for o in range(1, sectors):
        to = peer(0, o)
        send(gk.at[pl.ds(to["lon"] * kch, kch)], gkrecv.at[o - 1], 10, to)

    def adj_own_body(cs):
        acc = [cotr[j, cs, :] for j in range(TY)]
        acc = conv_own(gext, kb, cs, True, acc)
        for j in range(TY):
            conv[j, cs, :] = acc[j]

    each_tile(adj_own_body, 16)

    wait_bytes(partrecv, sems.at[11])
    own = part[pl.ds(pl.multiple_of(lon * wch, 16), wch), :].astype(F32)
    for o in range(1, sectors):
        own = own + partrecv[o - 1].astype(F32)
    total[0:wch, :] = own
    wait_bytes(gkrecv, sems.at[21])
    own = gk[pl.ds(pl.multiple_of(lon * kch, 8), kch), :]
    for o in range(1, sectors):
        own = own + gkrecv[o - 1]
    total[wch:chunk, :] = own
    if total.shape[0] > chunk:
        total[chunk:, :] = jnp.zeros((total.shape[0] - chunk, 128), F32)
    for o in range(1, bands):
        to = peer(o, 0)
        send(total.at[pl.ds(to["lat"] * piece, piece)], totalrecv.at[o - 1], 7, to)

    exchange(gsendrows, gsendedge, grecvrows, grecvedge, 3)

    @pl.when(is_north)
    def _():
        here = pl.ds(pl.multiple_of(lon * TX, TX), TX)
        for o in range(1, sectors):
            send(gsendrows.at[pl.ds(3 * C, 3 * C)], foldrecv2.at[:, here], 6, peer(0, o))
        foldrecv2[:, here] = gsendrows[3 * C :, :]

    mine = pl.ds(pl.multiple_of(lat * piece, 8), piece)
    acc = total[mine, :]
    wait_bytes(totalrecv, sems.at[15])
    for o in range(1, bands):
        acc = acc + totalrecv[o - 1]
    full[mine, :] = acc
    for o in range(1, bands):
        send(full.at[pl.ds(lat * piece, piece)], full.at[pl.ds(lat * piece, piece)], 8, peer(o, 0))
    fill_halo(grecvrows, grecvedge, gext, gedge, 3)

    def adj_halo_body(cs):
        acc = [conv[j, cs, :] for j in range(TY)]
        acc = conv_edge(gedge, kb, cs, True, acc, 0)
        acc = conv_halo(gext, kb, cs, True, acc, True, True)
        for j in range(TY):
            conv[j, cs, :] = acc[j]

    each_tile(adj_halo_body, 24)

    wait_bytes(full.at[pl.ds(0, (bands - 1) * piece)], sems.at[17])
    final[pl.ds(pl.multiple_of(lon * fch, 16), fch), :] = full[0:fch, :].astype(BF16)
    for o in range(1, sectors):
        send(final.at[pl.ds(lon * fch, fch)], final.at[pl.ds(lon * fch, fch)], 9, peer(0, o))

    @pl.when(is_north)
    def _():
        wait_bytes(foldrecv2.at[:, pl.ds(0, (sectors - 1) * TX)], sems.at[13])
        for r in range(3):
            near = dot_nt(foldrecv2[r * C : (r + 1) * C, :], onehot2[...])
            for k in range(r + 1):
                acc = conv[7 - k]
                for b in range(7):
                    acc = acc + kb[7 * (6 + k - r) + b] * near[:, b * TX : (b + 1) * TX]
                conv[7 - k] = acc

    for j in range(TY):
        grad_rows[j] = conv[j].astype(BF16)

    wait_bytes(final.at[pl.ds(0, (sectors - 1) * fch)], sems.at[19])
    sums_out[...] = final[...]

    wait_bytes(recvrows, sems.at[0])
    wait_bytes(recvedge, sems.at[2])
    wait_bytes(grecvrows, sems.at[6])
    wait_bytes(grecvedge, sems.at[8])
    wait_bytes(partrecv, sems.at[10])
    wait_bytes(gkrecv, sems.at[20])
    wait_bytes(totalrecv, sems.at[14])
    wait_bytes(totalrecv, sems.at[16])
    wait_bytes(final.at[pl.ds(0, (sectors - 1) * fch)], sems.at[18])

    @pl.when(is_north)
    def _():
        wait_bytes(foldrecv.at[pl.ds(0, (sectors - 1) * 3 * C)], sems.at[4])
        wait_bytes(foldrecv2.at[:, pl.ds(0, (sectors - 1) * TX)], sems.at[12])


def finish_kernel(
    sectors, out_rows, grad_rows, sums, out_field, grad_field, gkt, ge, gpt, nat
):
    wch = WROWS // sectors
    kch = C // sectors
    fch = sums.shape[0] // sectors
    for src, dst in ((out_rows, out_field), (grad_rows, grad_field)):
        for j in range(TY):
            nat[pl.ds(j, C, stride=TY), :] = src[j].astype(F32)
        dst[...] = nat[...].astype(BF16)
    blocks = HID // 128
    for b in range(2 * blocks):
        dst = ge if b < blocks else gpt
        lanes = slice((b % blocks) * 128, (b % blocks + 1) * 128)
        for r in range(0, C, PIECE):
            w = b * C + r
            at = (w // wch) * fch + w % wch
            dst[r : r + PIECE, lanes] = sums[at : at + PIECE, :].astype(F32)
    for n in range(sectors):
        at = n * fch + wch
        nat[n * kch : (n + 1) * kch, :] = sums[at : (n + 1) * fch, :].astype(F32)[:kch]
    gkt[...] = nat[0:C, :].T[:TAPS]


def on_device(
    bands,
    sectors,
    state_field,
    depth_kernel,
    norm_gain,
    w_expand,
    w_project,
    layer_scale,
    cotangent,
    send_cells,
    send_count,
    fold_partner,
):
    wch = WROWS // sectors
    kch = C // sectors
    fch = wch + -(-kch // 16) * 16
    piece = -(-fch // (8 * bands)) * 8
    vmem = pl.BlockSpec(memory_space=pltpu.VMEM)
    smem = pl.BlockSpec(memory_space=pltpu.SMEM)
    sds = jax.ShapeDtypeStruct
    rows3 = pltpu.VMEM((6 * C, 128), BF16)
    edge = pltpu.VMEM((6, GC, 128), BF16)
    fold = pltpu.VMEM((sectors * 3 * C, 128), BF16)
    scratch = dict(
        nat=pltpu.VMEM((C * TY, 128), F32),
        ext=pltpu.VMEM((EXT, C, 128), F32),
        gext=pltpu.VMEM((EXT, C, 128), F32),
        edge=pltpu.VMEM((C, 128), F32),
        gedge=pltpu.VMEM((C, 128), F32),
        packed=pltpu.VMEM((C, 128), F32),
        gpacked=pltpu.VMEM((C, 128), F32),
        cotr=pltpu.VMEM((TY, C, 128), F32),
        conv=pltpu.VMEM((TY, C, 128), F32),
        upstream=pltpu.VMEM((C, CELLS), BF16),
        scaled=pltpu.VMEM((C, CELLS), BF16),
        hidden=pltpu.VMEM((HID, CELLS), BF16),
        gradpre=pltpu.VMEM((HID, CELLS), BF16),
        wexpt=pltpu.VMEM((HID, C), BF16),
        w_project=pltpu.VMEM((HID, C), BF16),
        wet=pltpu.VMEM((TY, TX), F32),
        kb=pltpu.VMEM((TAPS, C, 128), F32),
        fedge=pltpu.VMEM((C, 128), F32),
        gk=pltpu.VMEM((C, 128), F32),
        sendrows=rows3,
        sendedge=pltpu.VMEM((2, GC, 128), BF16),
        recvrows=rows3,
        recvedge=edge,
        gsendrows=rows3,
        gsendedge=pltpu.VMEM((2, GC, 128), BF16),
        grecvrows=rows3,
        grecvedge=edge,
        foldrecv=fold,
        foldrecv2=pltpu.VMEM((3 * C, sectors * TX), BF16),
        onehot=pltpu.VMEM((sectors, TX, 2 * TX), BF16),
        onehot2=pltpu.VMEM((7 * TX, sectors * TX), BF16),
        part=pltpu.VMEM((WROWS, 128), BF16),
        partrecv=pltpu.VMEM((sectors - 1, wch, 128), BF16),
        gkrecv=pltpu.VMEM((sectors - 1, kch, 128), F32),
        total=pltpu.VMEM((bands * piece, 128), F32),
        totalrecv=pltpu.VMEM((bands - 1, piece, 128), F32),
        full=pltpu.VMEM((bands * piece, 128), F32),
        final=pltpu.VMEM((sectors * fch, 128), BF16),
        sems=pltpu.SemaphoreType.DMA((22,)),
    )
    out_rows, grad_rows, sums = pl.pallas_call(
        functools.partial(block_kernel, bands, sectors),
        out_shape=(
            sds((TY, C, 128), BF16),
            sds((TY, C, 128), BF16),
            sds((sectors * fch, 128), BF16),
        ),
        in_specs=[vmem] * 8 + [smem] + [vmem],
        out_specs=(vmem, vmem, vmem),
        scratch_shapes=list(scratch.values()),
        compiler_params=pltpu.CompilerParams(
            collective_id=0, has_side_effects=True, vmem_limit_bytes=48 * 2**20
        ),
        name="block",
    )(
        state_field.reshape(C * TY, TX),
        cotangent.reshape(C * TY, TX),
        depth_kernel.T,
        norm_gain.reshape(1, C),
        layer_scale.reshape(1, C),
        w_expand,
        w_project.T,
        send_cells,
        send_count,
        fold_partner.reshape(1, sectors * TX),
    )
    out_field, grad_field, gkt, ge, gpt = pl.pallas_call(
        functools.partial(finish_kernel, sectors),
        out_shape=(
            sds((C * TY, TX), BF16),
            sds((C * TY, TX), BF16),
            sds((TAPS, C), F32),
            sds((C, HID), F32),
            sds((C, HID), F32),
        ),
        in_specs=[vmem] * 3,
        out_specs=(vmem,) * 5,
        scratch_shapes=[pltpu.VMEM((C * TY, 128), F32)],
        compiler_params=pltpu.CompilerParams(vmem_limit_bytes=32 * 2**20),
        name="finish",
    )(out_rows, grad_rows, sums)
    return (
        out_field.reshape(C, TY, TX),
        grad_field.reshape(C, TY, TX),
        gkt.T,
        ge,
        gpt.T,
    )


def solution(mesh):
    return jax.shard_map(
        functools.partial(on_device, mesh.shape["lat"], mesh.shape["lon"]),
        mesh=mesh,
        in_specs=(
            P(None, "lat", "lon"),
            P(),
            P(),
            P(),
            P(),
            P(),
            P(None, "lat", "lon"),
            P("lat", "lon"),
            P("lat", "lon"),
            P(),
        ),
        out_specs=(P(None, "lat", "lon"), P(None, "lat", "lon"), P(), P(), P()),
        check_vma=False,
    )
```

time: 78.9 us -> 75.5 us (0.957)
  Pallas kernels: 73 us -> 69 us
    pallas_call x1, Pallas kernels: 71.5 us -> 67.3 us  [on_device(): pl.pallas_call(functools.partial(block_kernel, bands, sectors), out_shape...]
where the time goes in v2:
time: 75.5 us; the launch traced here: 75.2 us
  Pallas kernels  69 us (91%)
  local copies, waits for them, and re-layouts  5.43 us (7%)
    pallas_call x1, Pallas kernels, on_device(): pl.pallas_call(functools.partial(block_kernel, bands, sectors), out_shape...  67.3 us
    unnamed x20, local copies, waits for them, and re-layouts  5.43 us
    pallas_call x1, Pallas kernels, on_device(): pl.pallas_call(functools.partial(finish_kernel, sectors), out_shape=(sds(...  1.72 us

profile of v2, /device:TPU:1, one launch (start us, length us, event | category | flops | bytes accessed | tf_op | source)
XLA Modules:
  0.0 75.2 jit_solution(8544097691993430235)
XLA Ops:
  0.6 0.0 copy-start.8
  0.6 0.0 copy-start.9
  0.7 0.0 copy-start.6
  0.7 0.0 copy-start.5
  0.7 0.0 copy-start.7
  0.7 0.6 copy-done.8
  1.3 0.0 copy-done.9
  1.3 0.0 copy-done.6
  1.4 0.0 copy-done.5
  1.4 0.0 copy-done.7
  1.4 0.0 copy-start
  1.4 1.0 %copy-done = bf16[192,8,128]{2,1,0:T(8,128)(2,1)S(1)} copy-done((bf16[192,8,128]{2,1,0:T(8,128)(2,1)S(1)}, bf16[192,8,128]{2,1,0:T(8,128)(2,1)}, u32[]{:S(2)}) %copy-start) | copy-done | bytes 393240
  2.4 0.0 copy-start.1
  2.4 1.0 %copy-done.1 = bf16[192,8,128]{2,1,0:T(8,128)(2,1)S(1)} copy-done((bf16[192,8,128]{2,1,0:T(8,128)(2,1)S(1)}, bf16[192,8,128]{2,1,0:T(8,128)(2,1)}, u32[]{:S(2)}) %copy-start.1) | copy-done | bytes 393240
  3.4 0.0 copy-start.2
  3.4 1.0 %copy-done.2 = bf16[192,768]{1,0:T(8,128)(2,1)S(1)} copy-done((bf16[192,768]{1,0:T(8,128)(2,1)S(1)}, bf16[192,768]{1,0:T(8,128)(2,1)}, u32[]{:S(2)}) %copy-start.2) | copy-done | bytes 294936
  4.3 0.0 copy-start.3
  4.3 1.0 %copy-done.3 = bf16[768,192]{0,1:T(8,128)(2,1)S(1)} copy-done((bf16[768,192]{0,1:T(8,128)(2,1)S(1)}, bf16[768,192]{0,1:T(8,128)(2,1)}, u32[]{:S(2)}) %copy-start.3) | copy-done | bytes 294936
  5.3 0.0 copy-start.4
  5.3 0.8 %copy-done.4 = f32[192,49]{0,1:T(8,128)S(1)} copy-done((f32[192,49]{0,1:T(8,128)S(1)}, f32[192,49]{0,1:T(8,128)}, u32[]{:S(2)}) %copy-start.4) | copy-done | bytes 37656
  6.1 67.3 %block.1 = (bf16[8,192,128]{2,1,0:T(8,128)(2,1)S(1)}, bf16[8,192,128]{2,1,0:T(8,128)(2,1)S(1)}, bf16[2560,128]{1,0:T(8,128)(2,1)S(1)}) custom-call(bf16[1536,128]{1,0:T(8,128)(2,1)S(1)} %bitcast.11, bf16[1536,128]{1,0:T(8,128)(2,1)S(1)} %bitcast.12, f32[49,192]{1,0:T(8,128)S(1)} %bitcast.14, f32[1,192]{1,0:T(1,128)S(1)} %bitcast.16, f32[1,192]{1,0:T(1,128)S(1)} %bitcast.17, ...), custom_call_target="tpu_custom_call" | custom-call | tf_op jit(solution)/shard_map/block/pallas_call | solution.py:676
  73.4 1.7 %finish.1 = (bf16[1536,128]{1,0:T(8,128)(2,1)}, bf16[1536,128]{1,0:T(8,128)(2,1)}, f32[49,192]{1,0:T(8,128)}, f32[192,768]{1,0:T(8,128)}, f32[192,768]{1,0:T(8,128)}) custom-call(bf16[8,192,128]{2,1,0:T(8,128)(2,1)S(1)} %get-tuple-element.13.out_rows, bf16[8,192,128]{2,1,0:T(8,128)(2,1)S(1)} %get-tuple-element.14.grad_rows, ...), custom_call_target="tpu_custom_call" | custom-call | tf_op jit(solution)/shard_map/finish/pallas_call | solution.py:702
Async XLA Ops:
  0.6 0.7 copy-start.8
  0.6 0.7 copy-start.9
  0.7 0.7 copy-start.6
  0.7 0.7 copy-start.5
  0.7 0.7 copy-start.7
  1.4 1.0 %copy-start = (bf16[192,8,128]{2,1,0:T(8,128)(2,1)S(1)}, bf16[192,8,128]{2,1,0:T(8,128)(2,1)}, u32[]{:S(2)}) copy-start(bf16[192,8,128]{2,1,0:T(8,128)(2,1)} %param.10) | copy-start | bytes 1179652
  2.4 1.0 %copy-start.1 = (bf16[192,8,128]{2,1,0:T(8,128)(2,1)S(1)}, bf16[192,8,128]{2,1,0:T(8,128)(2,1)}, u32[]{:S(2)}) copy-start(bf16[192,8,128]{2,1,0:T(8,128)(2,1)} %param.16) | copy-start | bytes 1179652
  3.4 1.0 %copy-start.2 = (bf16[192,768]{1,0:T(8,128)(2,1)S(1)}, bf16[192,768]{1,0:T(8,128)(2,1)}, u32[]{:S(2)}) copy-start(bf16[192,768]{1,0:T(8,128)(2,1)} %w_expand.1) | copy-start | bytes 884740
  4.3 1.0 %copy-start.3 = (bf16[768,192]{0,1:T(8,128)(2,1)S(1)}, bf16[768,192]{0,1:T(8,128)(2,1)}, u32[]{:S(2)}) copy-start(bf16[768,192]{0,1:T(8,128)(2,1)} %param.14) | copy-start | bytes 884740
  5.3 0.8 %copy-start.4 = (f32[192,49]{0,1:T(8,128)S(1)}, f32[192,49]{0,1:T(8,128)}, u32[]{:S(2)}) copy-start(f32[192,49]{0,1:T(8,128)} %param.11) | copy-start | bytes 112900

commit v3 on v2

--- a/solution.py
+++ b/solution.py
@@ -189,18 +189,18 @@
 def block_kernel(
     bands,
     sectors,
-    state,
-    cot,
-    dkt,
-    gain,
-    lscale,
-    w_expand,
-    wprojt,
-    cells,
+    state_in,
+    cot_in,
+    dkt_in,
+    gain_in,
+    lscale_in,
+    w_expand_in,
+    wprojt_in,
+    cells_in,
     counts,
-    partner,
-    out_rows,
-    grad_rows,
+    partner_in,
+    out_nat,
+    grad_nat,
     sums_out,
     nat,
     ext,
@@ -235,16 +235,30 @@
     onehot2,
     part,
     partrecv,
+    gkparts,
     gkrecv,
+    gksum,
+    gkall,
     total,
     totalrecv,
     full,
     final,
     sems,
+    state,
+    cot,
+    dkt,
+    gain,
+    lscale,
+    w_expand,
+    wprojt,
+    cells,
+    partner,
+    out_field,
+    grad_field,
+    loads,
 ):
     wch = WROWS // sectors
     kch = C // sectors
-    chunk = wch + kch
     fch = final.shape[0] // sectors
     piece = totalrecv.shape[1]
     lat = lax.axis_index("lat")
@@ -269,12 +283,30 @@
         )
         cp.start()
 
+    sources = (
+        (state_in, state),
+        (dkt_in, dkt),
+        (cot_in, cot),
+        (w_expand_in, w_expand),
+        (wprojt_in, wprojt),
+        (gain_in, gain),
+        (lscale_in, lscale),
+        (cells_in, cells),
+        (partner_in, partner),
+    )
+    copies = [
+        pltpu.make_async_copy(src, dst, loads.at[n]) for n, (src, dst) in enumerate(sources)
+    ]
+    for cp in copies:
+        cp.start()
+
     barrier = pltpu.get_barrier_semaphore()
     peers = [(o, 0) for o in range(1, bands)] + [(0, o) for o in range(1, sectors)]
     peers += [(1, 1), (1, -1), (-1, 1), (-1, -1)]
     for dlat, dlon in peers:
         pl.semaphore_signal(barrier, inc=1, device_id=peer(dlat, dlon), device_id_type=MESH)
 
+    copies[0].wait()
     nat[...] = state[...].astype(F32)
     for j in range(TY):
         ext[3 + j] = nat[pl.ds(j, C, stride=TY), :]
@@ -282,6 +314,30 @@
         sendrows[k * C : (k + 1) * C, :] = ext[3 + j].astype(BF16)
     pack_edges(ext, packed)
     edge_messages(packed, sendedge.at[0], sendedge.at[1])
+
+    pl.semaphore_wait(barrier, len(peers))
+
+    def exchange(rows_s, edge_s, rows_r, edge_r, s):
+        for n, dlat in enumerate((1, 0, -1)):
+            send(edge_s.at[1], edge_r.at[n], s + 1, peer(dlat, 1))
+            send(edge_s.at[0], edge_r.at[3 + n], s + 1, peer(dlat, -1))
+        send(rows_s.at[pl.ds(0, 3 * C)], rows_r.at[pl.ds(3 * C, 3 * C)], s, peer(-1, 0))
+        send(rows_s.at[pl.ds(3 * C, 3 * C)], rows_r.at[pl.ds(0, 3 * C)], s, peer(1, 0))
+
+    exchange(sendrows, sendedge, recvrows, recvedge, 0)
+
+    @pl.when(is_north)
+    def _():
+        for o in range(1, sectors):
+            send(
+                sendrows.at[pl.ds(3 * C, 3 * C)],
+                foldrecv.at[pl.ds(lon * (3 * C), 3 * C)],
+                2,
+                peer(0, o),
+            )
+
+    for cp in copies[1:]:
+        cp.wait()
 
     seg = lax.broadcasted_iota(jnp.int32, (1, CELLS), 1)
     capacity = CELLS // bands
@@ -299,27 +355,6 @@
     dkp = jnp.concatenate([dkt[...], jnp.zeros((128 - TAPS, C), F32)], axis=0).T
     for t in range(TAPS):
         kb[t] = jnp.broadcast_to(dkp[:, t : t + 1], (C, 128))
-
-    pl.semaphore_wait(barrier, len(peers))
-
-    def exchange(rows_s, edge_s, rows_r, edge_r, s):
-        for n, dlat in enumerate((1, 0, -1)):
-            send(edge_s.at[1], edge_r.at[n], s + 1, peer(dlat, 1))
-            send(edge_s.at[0], edge_r.at[3 + n], s + 1, peer(dlat, -1))
-        send(rows_s.at[pl.ds(0, 3 * C)], rows_r.at[pl.ds(3 * C, 3 * C)], s, peer(-1, 0))
-        send(rows_s.at[pl.ds(3 * C, 3 * C)], rows_r.at[pl.ds(0, 3 * C)], s, peer(1, 0))
-
-    exchange(sendrows, sendedge, recvrows, recvedge, 0)
-
-    @pl.when(is_north)
-    def _():
-        for o in range(1, sectors):
-            send(
-                sendrows.at[pl.ds(3 * C, 3 * C)],
-                foldrecv.at[pl.ds(lon * (3 * C), 3 * C)],
-                2,
-                peer(0, o),
-            )
 
     gain_c = column(gain)
     scale_c = column(lscale)
@@ -417,7 +452,7 @@
             half_at = slice(n * TX, (n + 1) * TX)
             j = 2 * m + n
             b = wet[pl.ds(j, 1), :] * scale_c * branch[:, half_at]
-            out_rows[j] = (ext[3 + j] + b).astype(BF16)
+            nat[pl.ds(j, C, stride=TY), :] = ext[3 + j] + b
             gext[3 + j] = gr[:, half_at]
         return carry
 
@@ -466,6 +501,10 @@
         to = peer(0, o)
         send(part.at[pl.ds(to["lon"] * wch, wch)], partrecv.at[o - 1], 5, to)
 
+    out_field[...] = nat[...].astype(BF16)
+    out_copy = pltpu.make_async_copy(out_field, out_nat, loads.at[0])
+    out_copy.start()
+
     for k, j in enumerate((0, 1, 2, 5, 6, 7)):
         gsendrows[k * C : (k + 1) * C, :] = gext[3 + j].astype(BF16)
     pack_edges(gext, gpacked)
@@ -477,7 +516,6 @@
         terms = edge_terms(edge, cs)
         gp = gpacked[cs, :]
         beside = [turn(gp, 4 * a) for a in range(7)]
-        res = jnp.zeros((cs.size, 128), F32)
         for d in range(7):
             y = shifted(g, 6 - d)
             for a in range(7):
@@ -486,34 +524,31 @@
                     v = v + jnp.where(lane < 64, terms[d] * beside[a], 0.0)
                 if d > 3:
                     v = v + jnp.where(lane >= 64, terms[6 - d] * beside[a], 0.0)
-                res = jnp.where(lane == 7 * a + d, jnp.sum(v, axis=1, keepdims=True), res)
-        gk[cs, :] = res
-
-    each_tile(gk_body, 16)
+                gkparts[7 * a + d, cs, :] = v
+
+    each_tile(gk_body, 8)
+    lane = lax.broadcasted_iota(jnp.int32, (C, 128), 1)
+    ones = jnp.ones((128, 128), BF16)
+    res = jnp.zeros((C, 128), F32)
+    for a in range(7):
+        v = gkparts[7 * a : 7 * a + 7].reshape(7 * C, 128)
+        hi = v.astype(BF16)
+        lo = (v - hi.astype(F32)).astype(BF16)
+        v = dot_nn(hi, ones) + dot_nn(lo, ones)
+        for d in range(7):
+            res = jnp.where(lane == 7 * a + d, v[d * C : (d + 1) * C], res)
+    gk[...] = res
     for o in range(1, sectors):
         to = peer(0, o)
         send(gk.at[pl.ds(to["lon"] * kch, kch)], gkrecv.at[o - 1], 10, to)
-
-    def adj_own_body(cs):
-        acc = [cotr[j, cs, :] for j in range(TY)]
-        acc = conv_own(gext, kb, cs, True, acc)
-        for j in range(TY):
-            conv[j, cs, :] = acc[j]
-
-    each_tile(adj_own_body, 16)
 
     wait_bytes(partrecv, sems.at[11])
     own = part[pl.ds(pl.multiple_of(lon * wch, 16), wch), :].astype(F32)
     for o in range(1, sectors):
         own = own + partrecv[o - 1].astype(F32)
     total[0:wch, :] = own
-    wait_bytes(gkrecv, sems.at[21])
-    own = gk[pl.ds(pl.multiple_of(lon * kch, 8), kch), :]
-    for o in range(1, sectors):
-        own = own + gkrecv[o - 1]
-    total[wch:chunk, :] = own
-    if total.shape[0] > chunk:
-        total[chunk:, :] = jnp.zeros((total.shape[0] - chunk, 128), F32)
+    if total.shape[0] > wch:
+        total[wch:, :] = jnp.zeros((total.shape[0] - wch, 128), F32)
     for o in range(1, bands):
         to = peer(o, 0)
         send(total.at[pl.ds(to["lat"] * piece, piece)], totalrecv.at[o - 1], 7, to)
@@ -526,6 +561,14 @@
         for o in range(1, sectors):
             send(gsendrows.at[pl.ds(3 * C, 3 * C)], foldrecv2.at[:, here], 6, peer(0, o))
         foldrecv2[:, here] = gsendrows[3 * C :, :]
+
+    wait_bytes(gkrecv, sems.at[21])
+    own = gk[pl.ds(pl.multiple_of(lon * kch, 8), kch), :]
+    for o in range(1, sectors):
+        own = own + gkrecv[o - 1]
+    gksum[...] = own
+    for o in range(1, bands):
+        send(gksum, gkall.at[o - 1], 11, peer(o, 0))
 
     mine = pl.ds(pl.multiple_of(lat * piece, 8), piece)
     acc = total[mine, :]
@@ -535,6 +578,26 @@
     full[mine, :] = acc
     for o in range(1, bands):
         send(full.at[pl.ds(lat * piece, piece)], full.at[pl.ds(lat * piece, piece)], 8, peer(o, 0))
+    def adj_own_body(cs):
+        acc = [cotr[j, cs, :] for j in range(TY)]
+        acc = conv_own(gext, kb, cs, True, acc)
+        for j in range(TY):
+            conv[j, cs, :] = acc[j]
+
+    each_tile(adj_own_body, 16)
+
+    wait_bytes(full.at[pl.ds(0, (bands - 1) * piece)], sems.at[17])
+    base = pl.multiple_of(lon * fch, 16)
+    final[pl.ds(base, wch), :] = full[0:wch, :].astype(BF16)
+    wait_bytes(gkall, sems.at[23])
+    own = gksum[...]
+    for o in range(1, bands):
+        own = own + gkall[o - 1]
+    tail = jnp.zeros((fch - wch - kch, 128), F32)
+    final[pl.ds(base + wch, fch - wch), :] = jnp.concatenate([own, tail], axis=0).astype(BF16)
+    for o in range(1, sectors):
+        send(final.at[pl.ds(lon * fch, fch)], final.at[pl.ds(lon * fch, fch)], 9, peer(0, o))
+
     fill_halo(grecvrows, grecvedge, gext, gedge, 3)
 
     def adj_halo_body(cs):
@@ -545,11 +608,6 @@
             conv[j, cs, :] = acc[j]
 
     each_tile(adj_halo_body, 24)
-
-    wait_bytes(full.at[pl.ds(0, (bands - 1) * piece)], sems.at[17])
-    final[pl.ds(pl.multiple_of(lon * fch, 16), fch), :] = full[0:fch, :].astype(BF16)
-    for o in range(1, sectors):
-        send(final.at[pl.ds(lon * fch, fch)], final.at[pl.ds(lon * fch, fch)], 9, peer(0, o))
 
     @pl.when(is_north)
     def _():
@@ -563,17 +621,25 @@
                 conv[7 - k] = acc
 
     for j in range(TY):
-        grad_rows[j] = conv[j].astype(BF16)
+        nat[pl.ds(j, C, stride=TY), :] = conv[j]
+    grad_field[...] = nat[...].astype(BF16)
+    grad_copy = pltpu.make_async_copy(grad_field, grad_nat, loads.at[1])
+    grad_copy.start()
 
     wait_bytes(final.at[pl.ds(0, (sectors - 1) * fch)], sems.at[19])
-    sums_out[...] = final[...]
-
+    sums_copy = pltpu.make_async_copy(final, sums_out, loads.at[2])
+    sums_copy.start()
+
+    out_copy.wait()
+    grad_copy.wait()
+    sums_copy.wait()
     wait_bytes(recvrows, sems.at[0])
     wait_bytes(recvedge, sems.at[2])
     wait_bytes(grecvrows, sems.at[6])
     wait_bytes(grecvedge, sems.at[8])
     wait_bytes(partrecv, sems.at[10])
     wait_bytes(gkrecv, sems.at[20])
+    wait_bytes(gkall, sems.at[22])
     wait_bytes(totalrecv, sems.at[14])
     wait_bytes(totalrecv, sems.at[16])
     wait_bytes(final.at[pl.ds(0, (sectors - 1) * fch)], sems.at[18])
@@ -585,27 +651,55 @@
 
 
 def finish_kernel(
-    sectors, out_rows, grad_rows, sums, out_field, grad_field, gkt, ge, gpt, nat
+    sectors,
+    out_nat,
+    grad_nat,
+    sums_in,
+    out_field,
+    grad_field,
+    gkt,
+    ge_out,
+    gpt_out,
+    gk,
+    sums,
+    fields,
+    ge,
+    gpt,
+    sems,
 ):
     wch = WROWS // sectors
     kch = C // sectors
     fch = sums.shape[0] // sectors
-    for src, dst in ((out_rows, out_field), (grad_rows, grad_field)):
-        for j in range(TY):
-            nat[pl.ds(j, C, stride=TY), :] = src[j].astype(F32)
-        dst[...] = nat[...].astype(BF16)
+    load = pltpu.make_async_copy(sums_in, sums, sems.at[2])
+    load.start()
+    loads = [
+        pltpu.make_async_copy(src, fields.at[n], sems.at[n])
+        for n, src in enumerate((out_nat, grad_nat))
+    ]
+    for cp in loads:
+        cp.start()
+    load.wait()
+    stores = []
     blocks = HID // 128
-    for b in range(2 * blocks):
-        dst = ge if b < blocks else gpt
-        lanes = slice((b % blocks) * 128, (b % blocks + 1) * 128)
-        for r in range(0, C, PIECE):
-            w = b * C + r
-            at = (w // wch) * fch + w % wch
-            dst[r : r + PIECE, lanes] = sums[at : at + PIECE, :].astype(F32)
+    for n, (dst, out) in enumerate(((ge, ge_out), (gpt, gpt_out))):
+        for b in range(blocks):
+            lanes = slice(b * 128, (b + 1) * 128)
+            for r in range(0, C, PIECE):
+                w = (n * blocks + b) * C + r
+                at = (w // wch) * fch + w % wch
+                dst[r : r + PIECE, lanes] = sums[at : at + PIECE, :].astype(F32)
+        stores.append(pltpu.make_async_copy(dst, out, sems.at[3 + n]))
+        stores[-1].start()
+    for n, (cp, dst) in enumerate(zip(loads, (out_field, grad_field))):
+        cp.wait()
+        stores.append(pltpu.make_async_copy(fields.at[n], dst, sems.at[5 + n]))
+        stores[-1].start()
     for n in range(sectors):
         at = n * fch + wch
-        nat[n * kch : (n + 1) * kch, :] = sums[at : (n + 1) * fch, :].astype(F32)[:kch]
-    gkt[...] = nat[0:C, :].T[:TAPS]
+        gk[n * kch : (n + 1) * kch, :] = sums[at : (n + 1) * fch, :].astype(F32)[:kch]
+    gkt[...] = gk[...].T[:TAPS]
+    for cp in stores:
+        cp.wait()
 
 
 def on_device(
@@ -625,8 +719,9 @@
     wch = WROWS // sectors
     kch = C // sectors
     fch = wch + -(-kch // 16) * 16
-    piece = -(-fch // (8 * bands)) * 8
+    piece = -(-wch // (8 * bands)) * 8
     vmem = pl.BlockSpec(memory_space=pltpu.VMEM)
+    hbm = pl.BlockSpec(memory_space=pltpu.HBM)
     smem = pl.BlockSpec(memory_space=pltpu.SMEM)
     sds = jax.ShapeDtypeStruct
     rows3 = pltpu.VMEM((6 * C, 128), BF16)
@@ -666,25 +761,40 @@
         onehot2=pltpu.VMEM((7 * TX, sectors * TX), BF16),
         part=pltpu.VMEM((WROWS, 128), BF16),
         partrecv=pltpu.VMEM((sectors - 1, wch, 128), BF16),
+        gkparts=pltpu.VMEM((TAPS, C, 128), F32),
         gkrecv=pltpu.VMEM((sectors - 1, kch, 128), F32),
+        gksum=pltpu.VMEM((kch, 128), F32),
+        gkall=pltpu.VMEM((bands - 1, kch, 128), F32),
         total=pltpu.VMEM((bands * piece, 128), F32),
         totalrecv=pltpu.VMEM((bands - 1, piece, 128), F32),
         full=pltpu.VMEM((bands * piece, 128), F32),
         final=pltpu.VMEM((sectors * fch, 128), BF16),
-        sems=pltpu.SemaphoreType.DMA((22,)),
+        sems=pltpu.SemaphoreType.DMA((24,)),
+        state=pltpu.VMEM((C * TY, TX), BF16),
+        cot=pltpu.VMEM((C * TY, TX), BF16),
+        dkt=pltpu.VMEM((TAPS, C), F32),
+        gain=pltpu.VMEM((1, C), F32),
+        lscale=pltpu.VMEM((1, C), F32),
+        w_expand=pltpu.VMEM((C, HID), BF16),
+        wprojt=pltpu.VMEM((C, HID), BF16),
+        cells=pltpu.VMEM((1, CELLS), jnp.int32),
+        partner=pltpu.VMEM((1, sectors * TX), jnp.int32),
+        out_field=pltpu.VMEM((C * TY, TX), BF16),
+        grad_field=pltpu.VMEM((C * TY, TX), BF16),
+        loads=pltpu.SemaphoreType.DMA((9,)),
     )
-    out_rows, grad_rows, sums = pl.pallas_call(
+    out_nat, grad_nat, sums = pl.pallas_call(
         functools.partial(block_kernel, bands, sectors),
         out_shape=(
-            sds((TY, C, 128), BF16),
-            sds((TY, C, 128), BF16),
+            sds((C * TY, TX), BF16),
+            sds((C * TY, TX), BF16),
             sds((sectors * fch, 128), BF16),
         ),
-        in_specs=[vmem] * 8 + [smem] + [vmem],
-        out_specs=(vmem, vmem, vmem),
+        in_specs=[hbm] * 8 + [smem] + [hbm],
+        out_specs=(hbm, hbm, hbm),
         scratch_shapes=list(scratch.values()),
         compiler_params=pltpu.CompilerParams(
-            collective_id=0, has_side_effects=True, vmem_limit_bytes=48 * 2**20
+            collective_id=0, has_side_effects=True, vmem_limit_bytes=60 * 2**20
         ),
         name="block",
     )(
@@ -708,12 +818,19 @@
             sds((C, HID), F32),
             sds((C, HID), F32),
         ),
-        in_specs=[vmem] * 3,
-        out_specs=(vmem,) * 5,
-        scratch_shapes=[pltpu.VMEM((C * TY, 128), F32)],
-        compiler_params=pltpu.CompilerParams(vmem_limit_bytes=32 * 2**20),
+        in_specs=[hbm, hbm, hbm],
+        out_specs=(hbm, hbm, vmem, hbm, hbm),
+        scratch_shapes=[
+            pltpu.VMEM((C, 128), F32),
+            pltpu.VMEM((sectors * fch, 128), BF16),
+            pltpu.VMEM((2, C * TY, TX), BF16),
+            pltpu.VMEM((C, HID), F32),
+            pltpu.VMEM((C, HID), F32),
+            pltpu.SemaphoreType.DMA((7,)),
+        ],
+        compiler_params=pltpu.CompilerParams(vmem_limit_bytes=60 * 2**20),
         name="finish",
-    )(out_rows, grad_rows, sums)
+    )(out_nat, grad_nat, sums)
     return (
         out_field.reshape(C, TY, TX),
         grad_field.reshape(C, TY, TX),

time: 75.5 us -> 69.7 us (0.923)
  local copies, waits for them, and re-layouts: 5.43 us -> 0 us
    unnamed x20 -> x0, local copies, waits for them, and re-layouts: 5.43 us -> none
    pallas_call x1, Pallas kernels: 67.3 us -> 65.8 us  [on_device(): pl.pallas_call(functools.partial(block_kernel, bands, sectors), out_shape...]
    pallas_call x1, Pallas kernels: 1.72 us -> 3.07 us  [on_device(): pl.pallas_call(functools.partial(finish_kernel, sectors), out_shape=(sds(...]
where the time goes in v3:
time: 69.7 us; the launch traced here: 69.5 us
  Pallas kernels  68.9 us (99%)
    pallas_call x1, Pallas kernels, on_device(): pl.pallas_call(functools.partial(block_kernel, bands, sectors), out_shape...  65.8 us
    pallas_call x1, Pallas kernels, on_device(): pl.pallas_call(functools.partial(finish_kernel, sectors), out_shape=(sds(...  3.07 us

profile of v3, /device:TPU:1, one launch (start us, length us, event | category | flops | bytes accessed | tf_op | source)
XLA Modules:
  0.0 69.5 jit_solution(1879715154626499709)
XLA Ops:
  0.6 65.8 %block.1 = (bf16[1536,128]{1,0:T(8,128)(2,1)}, bf16[1536,128]{1,0:T(8,128)(2,1)}, bf16[2560,128]{1,0:T(8,128)(2,1)}) custom-call(bf16[1536,128]{1,0:T(8,128)(2,1)} %bitcast.11, bf16[1536,128]{1,0:T(8,128)(2,1)} %bitcast.12, f32[49,192]{1,0:T(8,128)} %bitcast.14, f32[1,192]{1,0:T(1,128)} %bitcast.16, f32[1,192]{1,0:T(1,128)} %bitcast.17, ...), custom_call_target="tpu_custom_call" | custom-call | tf_op jit(solution)/shard_map/block/pallas_call | solution.py:786
  66.4 3.1 %finish.1 = (bf16[1536,128]{1,0:T(8,128)(2,1)}, bf16[1536,128]{1,0:T(8,128)(2,1)}, f32[49,192]{1,0:T(8,128)}, f32[192,768]{1,0:T(8,128)}, f32[192,768]{1,0:T(8,128)}) custom-call(bf16[1536,128]{1,0:T(8,128)(2,1)} %get-tuple-element.13.out_nat, bf16[1536,128]{1,0:T(8,128)(2,1)} %get-tuple-element.14.grad_nat, bf16[2560,128]{1,0:T(8,128)(2,1)} %get-tuple-element.15.sums_in), custom_call_target="tpu_custom_call" | custom-call | tf_op jit(solution)/shard_map/finish/pallas_call | solution.py:812

commit v4 on v3

--- a/solution.py
+++ b/solution.py
@@ -23,7 +23,7 @@
 GROUPS = 4
 GC = C // GROUPS
 WROWS = 2 * C * HID // 128
-PIECE = 96
+PIECE = 48
 
 
 def dot_nn(a, b):
@@ -234,6 +234,8 @@
     onehot,
     onehot2,
     part,
+    besiderecv,
+    halfsum,
     partrecv,
     gkparts,
     gkrecv,
@@ -257,12 +259,16 @@
     grad_field,
     loads,
 ):
-    wch = WROWS // sectors
+    half_rows = WROWS // 2
+    wch = half_rows // sectors
     kch = C // sectors
-    fch = final.shape[0] // sectors
+    fch = final.shape[0] // (2 * sectors)
+    chips = bands // 2
     piece = totalrecv.shape[1]
     lat = lax.axis_index("lat")
     lon = lax.axis_index("lon")
+    core = lax.rem(lat, 2)
+    chip = lat // 2
     is_south = lat == 0
     is_north = lat == bands - 1
 
@@ -271,6 +277,8 @@
             "lat": lax.rem(lat + (dlat + bands), bands),
             "lon": lax.rem(lon + (dlon + sectors), sectors),
         }
+
+    beside = {"lat": lat + 1 - 2 * core, "lon": lon}
 
     def send(src, dst, s, device):
         cp = pltpu.make_async_remote_copy(
@@ -491,24 +499,36 @@
     each_tile(north_body, 24)
     lax.fori_loop(TY // 4, TY // 2, mlp_body, 0)
 
+    for k, j in enumerate((0, 1, 2, 5, 6, 7)):
+        gsendrows[k * C : (k + 1) * C, :] = gext[3 + j].astype(BF16)
+
     ge = dot_nt(scaled[...], gradpre[...]).astype(BF16)
     gpt = dot_nt(upstream[...], hidden[...]).astype(BF16)
     blocks = HID // 128
     for b in range(blocks):
         part[b * C : (b + 1) * C, :] = ge[:, b * 128 : (b + 1) * 128]
         part[(blocks + b) * C : (blocks + b + 1) * C, :] = gpt[:, b * 128 : (b + 1) * 128]
-    for o in range(1, sectors):
-        to = peer(0, o)
-        send(part.at[pl.ds(to["lon"] * wch, wch)], partrecv.at[o - 1], 5, to)
-
+    send(part.at[pl.ds((1 - core) * half_rows, half_rows)], besiderecv, 12, beside)
     out_field[...] = nat[...].astype(BF16)
     out_copy = pltpu.make_async_copy(out_field, out_nat, loads.at[0])
     out_copy.start()
 
-    for k, j in enumerate((0, 1, 2, 5, 6, 7)):
-        gsendrows[k * C : (k + 1) * C, :] = gext[3 + j].astype(BF16)
     pack_edges(gext, gpacked)
     edge_messages(gpacked, gsendedge.at[0], gsendedge.at[1])
+    wait_bytes(besiderecv, sems.at[25])
+    half = part[pl.ds(pl.multiple_of(core * half_rows, 16), half_rows), :].astype(F32)
+    halfsum[...] = (half + besiderecv[...].astype(F32)).astype(BF16)
+    for o in range(1, sectors):
+        to = peer(0, o)
+        send(halfsum.at[pl.ds(to["lon"] * wch, wch)], partrecv.at[o - 1], 5, to)
+
+    @pl.when(is_north)
+    def _():
+        here = pl.ds(pl.multiple_of(lon * TX, TX), TX)
+        for o in range(1, sectors):
+            send(gsendrows.at[pl.ds(3 * C, 3 * C)], foldrecv2.at[:, here], 6, peer(0, o))
+        foldrecv2[:, here] = gsendrows[3 * C :, :]
+
     def gk_body(cs):
         lane = lax.broadcasted_iota(jnp.int32, (cs.size, 128), 1)
         x = ext[:, cs, :]
@@ -543,24 +563,17 @@
         send(gk.at[pl.ds(to["lon"] * kch, kch)], gkrecv.at[o - 1], 10, to)
 
     wait_bytes(partrecv, sems.at[11])
-    own = part[pl.ds(pl.multiple_of(lon * wch, 16), wch), :].astype(F32)
+    own = halfsum[pl.ds(pl.multiple_of(lon * wch, 16), wch), :].astype(F32)
     for o in range(1, sectors):
         own = own + partrecv[o - 1].astype(F32)
     total[0:wch, :] = own
     if total.shape[0] > wch:
         total[wch:, :] = jnp.zeros((total.shape[0] - wch, 128), F32)
-    for o in range(1, bands):
-        to = peer(o, 0)
-        send(total.at[pl.ds(to["lat"] * piece, piece)], totalrecv.at[o - 1], 7, to)
+    for o in range(1, chips):
+        to = peer(2 * o, 0)
+        send(total.at[pl.ds((to["lat"] // 2) * piece, piece)], totalrecv.at[o - 1], 7, to)
 
     exchange(gsendrows, gsendedge, grecvrows, grecvedge, 3)
-
-    @pl.when(is_north)
-    def _():
-        here = pl.ds(pl.multiple_of(lon * TX, TX), TX)
-        for o in range(1, sectors):
-            send(gsendrows.at[pl.ds(3 * C, 3 * C)], foldrecv2.at[:, here], 6, peer(0, o))
-        foldrecv2[:, here] = gsendrows[3 * C :, :]
 
     wait_bytes(gkrecv, sems.at[21])
     own = gk[pl.ds(pl.multiple_of(lon * kch, 8), kch), :]
@@ -570,14 +583,15 @@
     for o in range(1, bands):
         send(gksum, gkall.at[o - 1], 11, peer(o, 0))
 
-    mine = pl.ds(pl.multiple_of(lat * piece, 8), piece)
+    mine = pl.ds(pl.multiple_of(chip * piece, 8), piece)
     acc = total[mine, :]
     wait_bytes(totalrecv, sems.at[15])
-    for o in range(1, bands):
+    for o in range(1, chips):
         acc = acc + totalrecv[o - 1]
     full[mine, :] = acc
-    for o in range(1, bands):
-        send(full.at[pl.ds(lat * piece, piece)], full.at[pl.ds(lat * piece, piece)], 8, peer(o, 0))
+    piece_at = pl.ds(chip * piece, piece)
+    for o in range(1, chips):
+        send(full.at[piece_at], full.at[piece_at], 8, peer(2 * o, 0))
     def adj_own_body(cs):
         acc = [cotr[j, cs, :] for j in range(TY)]
         acc = conv_own(gext, kb, cs, True, acc)
@@ -586,8 +600,8 @@
 
     each_tile(adj_own_body, 16)
 
-    wait_bytes(full.at[pl.ds(0, (bands - 1) * piece)], sems.at[17])
-    base = pl.multiple_of(lon * fch, 16)
+    wait_bytes(full.at[pl.ds(0, (chips - 1) * piece)], sems.at[17])
+    base = pl.multiple_of((core * sectors + lon) * fch, 16)
     final[pl.ds(base, wch), :] = full[0:wch, :].astype(BF16)
     wait_bytes(gkall, sems.at[23])
     own = gksum[...]
@@ -595,8 +609,9 @@
         own = own + gkall[o - 1]
     tail = jnp.zeros((fch - wch - kch, 128), F32)
     final[pl.ds(base + wch, fch - wch), :] = jnp.concatenate([own, tail], axis=0).astype(BF16)
+    final_at = pl.ds((core * sectors + lon) * fch, fch)
     for o in range(1, sectors):
-        send(final.at[pl.ds(lon * fch, fch)], final.at[pl.ds(lon * fch, fch)], 9, peer(0, o))
+        send(final.at[final_at], final.at[final_at], 9, peer(0, o))
 
     fill_halo(grecvrows, grecvedge, gext, gedge, 3)
 
@@ -608,6 +623,10 @@
             conv[j, cs, :] = acc[j]
 
     each_tile(adj_halo_body, 24)
+
+    wait_bytes(final.at[pl.ds(0, (sectors - 1) * fch)], sems.at[19])
+    half_at = pl.ds(core * (sectors * fch), sectors * fch)
+    send(final.at[half_at], final.at[half_at], 13, beside)
 
     @pl.when(is_north)
     def _():
@@ -626,7 +645,7 @@
     grad_copy = pltpu.make_async_copy(grad_field, grad_nat, loads.at[1])
     grad_copy.start()
 
-    wait_bytes(final.at[pl.ds(0, (sectors - 1) * fch)], sems.at[19])
+    wait_bytes(final.at[pl.ds(0, sectors * fch)], sems.at[27])
     sums_copy = pltpu.make_async_copy(final, sums_out, loads.at[2])
     sums_copy.start()
 
@@ -639,6 +658,8 @@
     wait_bytes(grecvedge, sems.at[8])
     wait_bytes(partrecv, sems.at[10])
     wait_bytes(gkrecv, sems.at[20])
+    wait_bytes(besiderecv, sems.at[24])
+    wait_bytes(final.at[pl.ds(0, sectors * fch)], sems.at[26])
     wait_bytes(gkall, sems.at[22])
     wait_bytes(totalrecv, sems.at[14])
     wait_bytes(totalrecv, sems.at[16])
@@ -667,9 +688,10 @@
     gpt,
     sems,
 ):
-    wch = WROWS // sectors
+    half_rows = WROWS // 2
+    wch = half_rows // sectors
     kch = C // sectors
-    fch = sums.shape[0] // sectors
+    fch = sums.shape[0] // (2 * sectors)
     load = pltpu.make_async_copy(sums_in, sums, sems.at[2])
     load.start()
     loads = [
@@ -685,8 +707,8 @@
         for b in range(blocks):
             lanes = slice(b * 128, (b + 1) * 128)
             for r in range(0, C, PIECE):
-                w = (n * blocks + b) * C + r
-                at = (w // wch) * fch + w % wch
+                w = b * C + r
+                at = (n * sectors + w // wch) * fch + w % wch
                 dst[r : r + PIECE, lanes] = sums[at : at + PIECE, :].astype(F32)
         stores.append(pltpu.make_async_copy(dst, out, sems.at[3 + n]))
         stores[-1].start()
@@ -716,10 +738,11 @@
     send_count,
     fold_partner,
 ):
-    wch = WROWS // sectors
+    wch = WROWS // 2 // sectors
     kch = C // sectors
     fch = wch + -(-kch // 16) * 16
-    piece = -(-wch // (8 * bands)) * 8
+    chips = bands // 2
+    piece = -(-wch // (8 * chips)) * 8
     vmem = pl.BlockSpec(memory_space=pltpu.VMEM)
     hbm = pl.BlockSpec(memory_space=pltpu.HBM)
     smem = pl.BlockSpec(memory_space=pltpu.SMEM)
@@ -760,16 +783,18 @@
         onehot=pltpu.VMEM((sectors, TX, 2 * TX), BF16),
         onehot2=pltpu.VMEM((7 * TX, sectors * TX), BF16),
         part=pltpu.VMEM((WROWS, 128), BF16),
+        besiderecv=pltpu.VMEM((WROWS // 2, 128), BF16),
+        halfsum=pltpu.VMEM((WROWS // 2, 128), BF16),
         partrecv=pltpu.VMEM((sectors - 1, wch, 128), BF16),
         gkparts=pltpu.VMEM((TAPS, C, 128), F32),
         gkrecv=pltpu.VMEM((sectors - 1, kch, 128), F32),
         gksum=pltpu.VMEM((kch, 128), F32),
         gkall=pltpu.VMEM((bands - 1, kch, 128), F32),
-        total=pltpu.VMEM((bands * piece, 128), F32),
-        totalrecv=pltpu.VMEM((bands - 1, piece, 128), F32),
-        full=pltpu.VMEM((bands * piece, 128), F32),
-        final=pltpu.VMEM((sectors * fch, 128), BF16),
-        sems=pltpu.SemaphoreType.DMA((24,)),
+        total=pltpu.VMEM((chips * piece, 128), F32),
+        totalrecv=pltpu.VMEM((chips - 1, piece, 128), F32),
+        full=pltpu.VMEM((chips * piece, 128), F32),
+        final=pltpu.VMEM((2 * sectors * fch, 128), BF16),
+        sems=pltpu.SemaphoreType.DMA((28,)),
         state=pltpu.VMEM((C * TY, TX), BF16),
         cot=pltpu.VMEM((C * TY, TX), BF16),
         dkt=pltpu.VMEM((TAPS, C), F32),
@@ -788,7 +813,7 @@
         out_shape=(
             sds((C * TY, TX), BF16),
             sds((C * TY, TX), BF16),
-            sds((sectors * fch, 128), BF16),
+            sds((2 * sectors * fch, 128), BF16),
         ),
         in_specs=[hbm] * 8 + [smem] + [hbm],
         out_specs=(hbm, hbm, hbm),
@@ -822,7 +847,7 @@
         out_specs=(hbm, hbm, vmem, hbm, hbm),
         scratch_shapes=[
             pltpu.VMEM((C, 128), F32),
-            pltpu.VMEM((sectors * fch, 128), BF16),
+            pltpu.VMEM((2 * sectors * fch, 128), BF16),
             pltpu.VMEM((2, C * TY, TX), BF16),
             pltpu.VMEM((C, HID), F32),
             pltpu.VMEM((C, HID), F32),

time: 69.7 us -> 64.5 us (0.925)
  Pallas kernels: 68.9 us -> 63.7 us
    pallas_call x1, Pallas kernels: 65.8 us -> 60.6 us  [on_device(): pl.pallas_call(functools.partial(block_kernel, bands, sectors), out_shape...]
where the time goes in v4:
time: 64.5 us; the launch traced here: 64.3 us
  Pallas kernels  63.7 us (99%)
    pallas_call x1, Pallas kernels, on_device(): pl.pallas_call(functools.partial(block_kernel, bands, sectors), out_shape...  60.6 us
    pallas_call x1, Pallas kernels, on_device(): pl.pallas_call(functools.partial(finish_kernel, sectors), out_shape=(sds(...  3.09 us

profile of v4, /device:TPU:1, one launch (start us, length us, event | category | flops | bytes accessed | tf_op | source)
XLA Modules:
  0.0 64.3 jit_solution(9244204501176817427)
XLA Ops:
  0.6 60.6 %block.1 = (bf16[1536,128]{1,0:T(8,128)(2,1)}, bf16[1536,128]{1,0:T(8,128)(2,1)}, bf16[2816,128]{1,0:T(8,128)(2,1)}) custom-call(bf16[1536,128]{1,0:T(8,128)(2,1)} %bitcast.11, bf16[1536,128]{1,0:T(8,128)(2,1)} %bitcast.12, f32[49,192]{1,0:T(8,128)} %bitcast.14, f32[1,192]{1,0:T(1,128)} %bitcast.16, f32[1,192]{1,0:T(1,128)} %bitcast.17, ...), custom_call_target="tpu_custom_call" | custom-call | tf_op jit(solution)/shard_map/block/pallas_call | solution.py:811
  61.2 3.1 %finish.1 = (bf16[1536,128]{1,0:T(8,128)(2,1)}, bf16[1536,128]{1,0:T(8,128)(2,1)}, f32[49,192]{1,0:T(8,128)}, f32[192,768]{1,0:T(8,128)}, f32[192,768]{1,0:T(8,128)}) custom-call(bf16[1536,128]{1,0:T(8,128)(2,1)} %get-tuple-element.13.out_nat, bf16[1536,128]{1,0:T(8,128)(2,1)} %get-tuple-element.14.grad_nat, bf16[2816,128]{1,0:T(8,128)(2,1)} %get-tuple-element.15.sums_in), custom_call_target="tpu_custom_call" | custom-call | tf_op jit(solution)/shard_map/finish/pallas_call | solution.py:837

commit v5 on v4

--- a/solution.py
+++ b/solution.py
@@ -137,11 +137,11 @@
     return terms
 
 
-def edge_sums(edge, kb, cs, reverse, depth):
+def edge_sums(edge, kb, cs, reverse, offsets):
     left = slot_lanes((cs.size, 128), 0, 64)
     terms = edge_terms(edge, cs)
     total = None
-    for a in range(depth):
+    for a in offsets:
         y = None
         for s in range(3):
             lf = kb[tap(a, s, reverse), cs, :]
@@ -180,7 +180,7 @@
 
 
 def conv_edge(edge, kb, cs, reverse, acc, first):
-    total = edge_sums(edge, kb, cs, reverse, 7)
+    total = edge_sums(edge, kb, cs, reverse, range(4 if first else 0, 7))
     for j in range(first, TY):
         acc[j] = acc[j] + edge_row(total, j)
     return acc
@@ -234,6 +234,7 @@
     onehot,
     onehot2,
     part,
+    geh,
     besiderecv,
     halfsum,
     partrecv,
@@ -466,6 +467,10 @@
 
     lax.fori_loop(0, TY // 4, mlp_body, 0)
 
+    early = CELLS // 2
+    geh[0] = dot_nt(scaled[:, :early], gradpre[:, :early])
+    geh[1] = dot_nt(upstream[:, :early], hidden[:, :early])
+
     @pl.when(is_north)
     def _():
         wait_bytes(foldrecv.at[pl.ds(0, (sectors - 1) * 3 * C)], sems.at[5])
@@ -502,8 +507,8 @@
     for k, j in enumerate((0, 1, 2, 5, 6, 7)):
         gsendrows[k * C : (k + 1) * C, :] = gext[3 + j].astype(BF16)
 
-    ge = dot_nt(scaled[...], gradpre[...]).astype(BF16)
-    gpt = dot_nt(upstream[...], hidden[...]).astype(BF16)
+    ge = (geh[0] + dot_nt(scaled[:, early:], gradpre[:, early:])).astype(BF16)
+    gpt = (geh[1] + dot_nt(upstream[:, early:], hidden[:, early:])).astype(BF16)
     blocks = HID // 128
     for b in range(blocks):
         part[b * C : (b + 1) * C, :] = ge[:, b * 128 : (b + 1) * 128]
@@ -783,6 +788,7 @@
         onehot=pltpu.VMEM((sectors, TX, 2 * TX), BF16),
         onehot2=pltpu.VMEM((7 * TX, sectors * TX), BF16),
         part=pltpu.VMEM((WROWS, 128), BF16),
+        geh=pltpu.VMEM((2, C, HID), F32),
         besiderecv=pltpu.VMEM((WROWS // 2, 128), BF16),
         halfsum=pltpu.VMEM((WROWS // 2, 128), BF16),
         partrecv=pltpu.VMEM((sectors - 1, wch, 128), BF16),

time: 64.5 us -> 63.9 us (level)
  Pallas kernels: 63.7 us -> 63 us
    pallas_call x1, Pallas kernels: 60.6 us -> 60 us  [on_device(): pl.pallas_call(functools.partial(block_kernel, bands, sectors), out_shape...]
where the time goes in v5:
time: 63.9 us; the launch traced here: 63.7 us
  Pallas kernels  63 us (99%)
  between operations  0.64 us (1%)
    pallas_call x1, Pallas kernels, on_device(): pl.pallas_call(functools.partial(block_kernel, bands, sectors), out_shape...  60 us
    pallas_call x1, Pallas kernels, on_device(): pl.pallas_call(functools.partial(finish_kernel, sectors), out_shape=(sds(...  3.09 us

profile of v5, /device:TPU:1, one launch (start us, length us, event | category | flops | bytes accessed | tf_op | source)
XLA Modules:
  0.0 63.7 jit_solution(8132074376492646707)
XLA Ops:
  0.6 60.0 %block.1 = (bf16[1536,128]{1,0:T(8,128)(2,1)}, bf16[1536,128]{1,0:T(8,128)(2,1)}, bf16[2816,128]{1,0:T(8,128)(2,1)}) custom-call(bf16[1536,128]{1,0:T(8,128)(2,1)} %bitcast.11, bf16[1536,128]{1,0:T(8,128)(2,1)} %bitcast.12, f32[49,192]{1,0:T(8,128)} %bitcast.14, f32[1,192]{1,0:T(1,128)} %bitcast.16, f32[1,192]{1,0:T(1,128)} %bitcast.17, ...), custom_call_target="tpu_custom_call" | custom-call | tf_op jit(solution)/shard_map/block/pallas_call | solution.py:817
  60.6 3.1 %finish.1 = (bf16[1536,128]{1,0:T(8,128)(2,1)}, bf16[1536,128]{1,0:T(8,128)(2,1)}, f32[49,192]{1,0:T(8,128)}, f32[192,768]{1,0:T(8,128)}, f32[192,768]{1,0:T(8,128)}) custom-call(bf16[1536,128]{1,0:T(8,128)(2,1)} %get-tuple-element.13.out_nat, bf16[1536,128]{1,0:T(8,128)(2,1)} %get-tuple-element.14.grad_nat, bf16[2816,128]{1,0:T(8,128)(2,1)} %get-tuple-element.15.sums_in), custom_call_target="tpu_custom_call" | custom-call | tf_op jit(solution)/shard_map/finish/pallas_call | solution.py:843
